TPU v7x, 1024 devices: a whole 4x4x32 slice. The times are simulated.
1024 devices in a mesh: shard: 64 (over z_hi, y, x), replica: 16 (over z_lo, core).
Axes of the slice: x: 4, y: 4, z: 32 (z_hi: 4, z_lo: 8; z = z_hi * 8 + z_lo), core: 2. Of those that a mesh axis runs over, the one named last changes fastest.
Arguments:
- gradient: bfloat16 [16, 5120, 13824], P('replica', None, 'shard'), as said below
- projection: float32 [5120, 128], replicated, as said below
- first_moment: float32 [128, 13824], P(None, 'shard'), may hold values from -8 to 8
- second_moment: float32 [128, 13824], P(None, 'shard'), as said below
- weight: float32 [5120, 13824], P('replica', 'shard'), as said below
Outputs:
- update: float32 [5120, 13824], P('replica', 'shard')
- new_first: float32 [128, 13824], P(None, 'shard')
- new_second: float32 [128, 13824], P(None, 'shard')
Inputs may be any that keep to these rules, and one draw needn't show every extreme that they name: Real-valued gradient partials of order one. `projection`: Real-valued entries of order one over the square root of 5120. `second_moment`: positive entries. `weight`: Real-valued entries of order one.
All inputs are finite; a program needn't handle non-finite values.
Results may differ from a plain program's by a relative error of at most 0.0015.
The roundings to bfloat16 on the way count: a program that leaves them out, or rounds other values in their place, can miss the bound.
Values sent between devices are 32-bit elements; how exact they have to be, the bound alone decides.
No kernel may reach another device: no remote copies, remote signals or barrier semaphores. Data moves between devices by JAX's collectives and lax.ppermute only.
A program may use at most 32 MiB of HBM per device.

v0:
```python
import jax
import jax.numpy as jnp
from jax import lax
from jax.sharding import PartitionSpec as P

ADAM_STEP = 10


def adam_update(low_grad, first_moment, second_moment):
    new_first = 0.9 * first_moment + 0.1 * low_grad
    new_second = 0.95 * second_moment + 0.05 * low_grad * low_grad
    first_fix = 1.0 - 0.9**ADAM_STEP
    second_fix = 1.0 - 0.95**ADAM_STEP
    normalized = new_first / first_fix / (jnp.sqrt(new_second / second_fix) + 1e-08)
    return (new_first, new_second, normalized)


def shards(gradient, projection, first_moment, second_moment, weight):
    local_grad = gradient[0]
    low_projection = projection.astype(jnp.bfloat16)
    rank_total = projection.shape[1]
    rows_here = weight.shape[0]
    replicas = lax.axis_size("replica")
    position = lax.axis_index("replica")
    own_projection = lax.dynamic_slice_in_dim(projection, position * rows_here, rows_here, 0)
    share_rows = rank_total // replicas
    own_grad = lax.psum_scatter(
        lax.dot_general(
            low_projection, local_grad, (((0,), (0,)), ((), ())), preferred_element_type=jnp.float32
        ),
        "replica",
        scatter_dimension=0,
        tiled=True,
    )
    own_first = lax.dynamic_slice_in_dim(first_moment, position * share_rows, share_rows, 0)
    own_second = lax.dynamic_slice_in_dim(second_moment, position * share_rows, share_rows, 0)
    part_first, part_second, part_normal = adam_update(own_grad, own_first, own_second)
    piece_normal = lax.all_gather(part_normal, "replica", axis=0, tiled=True)
    piece_first = lax.all_gather(part_first, "replica", axis=0, tiled=True)
    piece_second = lax.all_gather(part_second, "replica", axis=0, tiled=True)
    step_sum = jnp.dot(
        own_projection,
        piece_normal,
        precision=lax.Precision.HIGHEST,
        preferred_element_type=jnp.float32,
    )
    weight_sq, step_sq = lax.psum(
        (jnp.sum(weight * weight), jnp.sum(step_sum * step_sum)), ("shard", "replica")
    )
    update = step_sum * (jnp.sqrt(weight_sq) / (jnp.sqrt(step_sq) + 1e-06))
    return (update, piece_first, piece_second)


def solution(mesh):
    placed = (
        P("replica", None, "shard"),
        P(),
        P(None, "shard"),
        P(None, "shard"),
        P("replica", "shard"),
    )
    return jax.shard_map(
        shards,
        mesh=mesh,
        in_specs=placed,
        out_specs=(P("replica", "shard"), P(None, "shard"), P(None, "shard")),
        check_vma=False,
    )
```

profile of v0, /device:TPU:1, one launch (start us, length us, event | category | flops | bytes accessed | tf_op | source)
XLA Modules:
  0.0 389.9 jit_solution(15535050715920291390)
XLA Ops:
  7.2 0.0 copy-start
  7.2 0.0 copy-start.3
  7.2 0.0 copy-start.2
  7.2 0.0 copy-start.1
  7.2 0.0 reduce-scatter.2.cloned.1.call-start
  7.3 1.5 copy-done
  8.8 3.2 fusion
  12.0 0.0 reduce-scatter.2.cloned.1.call-update
  12.0 0.0 copy-done.3
  12.0 0.0 copy-done.2
  12.1 0.1 constant_dynamic-slice_fusion
  12.2 0.1 copy.12
  12.2 0.1 copy.13
  12.3 0.0 copy-done.1
  12.3 0.7 multiply_reduce_fusion.1
  13.0 115.7 %reduce-scatter.2.cloned.1.call-done = f32[8,216]{1,0:T(8,128)} async-done(((f32[128,216]{1,0:T(8,128)}), f32[8,216]{1,0:T(8,128)}) %reduce-scatter.2.cloned.1.call-update) | async-done | bytes 6928 | tf_op jit(solution)/shard_map/reduce_scatter | solution.py:27
  128.7 0.7 add_divide_fusion
  129.4 32.1 %all_gather.9 = f32[128,216]{1,0:T(8,128)S(1)} all-gather(f32[8,216]{1,0:T(8,128)S(1)} %get-tuple-element.8), channel_id=1, replica_groups=mesh['shard'=64,'replica'=16] {'replica'}, dimensions={0}, use_global_device_ids=true | all-gather | bytes 117504 | tf_op jit(solution)/shard_map/all_gather | solution.py:38
  161.5 1.9 multiply_reduce_fusion
  163.4 156.4 %all-reduce = (f32[]{:T(128)}, f32[]{:T(128)}) all-reduce(f32[]{:T(128)} %multiply_reduce_fusion.1, f32[]{:T(128)} %get-tuple-element.11), channel_id=1, replica_groups=mesh['shard'=64,'replica'=16] {'shard','replica'}, use_global_device_ids=true, to_apply=%region_2.0 | all-reduce | flops 2 | bytes 16 | tf_op jit(solution)/shard_map/psum | solution.py:47
  321.2 33.8 %all_gather.10 = f32[128,216]{1,0:T(8,128)S(1)} all-gather(f32[8,216]{1,0:T(8,128)S(1)} %get-tuple-element.9), channel_id=1, replica_groups=mesh['shard'=64,'replica'=16] {'replica'}, dimensions={0}, use_global_device_ids=true | all-gather | bytes 117504 | tf_op jit(solution)/shard_map/all_gather | solution.py:39
  355.0 0.7 copy.10
  355.7 25.8 %all_gather.11 = f32[128,216]{1,0:T(8,128)S(1)} all-gather(f32[8,216]{1,0:T(8,128)S(1)} %get-tuple-element.10), channel_id=1, replica_groups=mesh['shard'=64,'replica'=16] {'replica'}, dimensions={0}, use_global_device_ids=true | all-gather | bytes 117504 | tf_op jit(solution)/shard_map/all_gather | solution.py:40
  381.5 0.7 copy.11
  382.3 0.7 broadcast_multiply_fusion
Async XLA Ops:
  7.2 1.6 copy-start
  7.2 4.9 %copy-start.3 = (f32[128,216]{0,1:T(8,128)S(1)}, f32[128,216]{0,1:T(8,128)}, u32[]{:S(2)}) copy-start(f32[128,216]{0,1:T(8,128)} %param.7) | copy-start | bytes 331780
  7.2 4.9 %copy-start.2 = (f32[128,216]{0,1:T(8,128)S(1)}, f32[128,216]{0,1:T(8,128)}, u32[]{:S(2)}) copy-start(f32[128,216]{0,1:T(8,128)} %param.8) | copy-start | bytes 331780
  7.2 5.1 %copy-start.1 = (f32[320,216]{1,0:T(8,128)S(1)}, f32[320,216]{1,0:T(8,128)}, u32[]{:S(2)}) copy-start(f32[320,216]{1,0:T(8,128)} %param.9) | copy-start | bytes 829444
  7.2 121.5 %reduce-scatter.2.cloned.1.call-start = ((), (), s32[]{:S(2)}) async-start(), calls=%async_computation.1 | async-start | bytes 139264 | tf_op jit(solution)/shard_map/reduce_scatter | solution.py:27
Sparse Core Ops, SparseCore 0:
  12.1 116.4 reduce-scatter.1
where the time goes:
time: 390 us
  blocking collectives  248 us (64%)
  waiting for transfers between devices  116 us (30%)
  between operations  15.5 us (4%)
  matrix products  5.14 us (1%)
    psum x1, blocking collectives, shards(): lax.psum((jnp.sum(weight * weight), jnp.sum(step_sum * step_sum)), ('shar...  156 us
    reduce_scatter x1, waiting for transfers between devices, shards(): lax.psum_scatter(lax.dot_general(low_projection, local_grad, (((0,), (0,)...  116 us
    all_gather x1, blocking collectives, shards(): piece_first = lax.all_gather(part_first, 'replica', axis=0, tiled=True)  33.8 us
    all_gather x1, blocking collectives, shards(): piece_normal = lax.all_gather(part_normal, 'replica', axis=0, tiled=True)  32.1 us
    all_gather x1, blocking collectives, shards(): piece_second = lax.all_gather(part_second, 'replica', axis=0, tiled=True)  25.8 us
  transfers between devices with their start and end apart: 1, of which 1 were waited for; matrix products, arithmetic and copies ran while one was open for 0% of the time, Pallas kernels for 0%

commit v1 on v0

v1 whole, which is shorter than its diff:
```python
import jax
import jax.numpy as jnp
from jax import lax
from jax.sharding import Mesh, PartitionSpec as P

ADAM_STEP = 10
SHARD = ("h1", "h0", "y1", "y0", "x1", "x0")
REPLICA = ("l2", "l1", "l0", "c")


def adam_update(low_grad, first_moment, second_moment):
    new_first = 0.9 * first_moment + 0.1 * low_grad
    new_second = 0.95 * second_moment + 0.05 * low_grad * low_grad
    first_fix = 1.0 - 0.9**ADAM_STEP
    second_fix = 1.0 - 0.95**ADAM_STEP
    normalized = new_first / first_fix / (jnp.sqrt(new_second / second_fix) + 1e-08)
    return (new_first, new_second, normalized)


def pair_sum(x, axis):
    both = lax.all_gather(x, axis, axis=0, tiled=False)
    return both[0] + both[1]


def shards(gradient, projection, first_moment, second_moment, weight):
    rows_here, columns = weight.shape
    rank = projection.shape[1]
    low_projection = projection.astype(jnp.bfloat16)
    partial = lax.dot_general(
        low_projection, gradient[0], (((0,), (0,)), ((), ())), preferred_element_type=jnp.float32
    )
    weight_part = jnp.sum(weight * weight)
    total = jnp.concatenate([partial, jnp.broadcast_to(weight_part, (rank, 256 - columns))], axis=1)
    for axis in ("c", "l0", "l1", "l2"):
        total = pair_sum(total, axis)
    low_grad = total[:, :columns]
    new_first, new_second, normalized = adam_update(low_grad, first_moment, second_moment)

    position = lax.axis_index(REPLICA)
    own_projection = lax.dynamic_slice_in_dim(projection, position * rows_here, rows_here, 0)
    step = jnp.dot(
        own_projection, normalized, precision=lax.Precision.HIGHEST, preferred_element_type=jnp.float32
    )
    shard_step = jnp.dot(
        projection, normalized, precision=lax.Precision.HIGH, preferred_element_type=jnp.float32
    )
    step_part = jnp.sum(shard_step * shard_step)
    lane = lax.broadcasted_iota(jnp.int32, (1, 128), 1)
    message = jnp.where(lane == 0, step_part, total[:1, 128:])
    shards_total = lax.axis_size(SHARD)
    parts = lax.all_to_all(
        jnp.broadcast_to(message[None], (shards_total, 1, 128)), SHARD, 0, 0
    )
    sums = jnp.sum(parts, axis=(0, 1))
    scale = jnp.sqrt(sums[127]) / (jnp.sqrt(sums[0]) + 1e-06)
    return (step * scale, new_first, new_second)


def solution(mesh):
    fine = Mesh(mesh.devices.reshape((2,) * 10), SHARD + REPLICA)
    placed = (
        P(REPLICA, None, SHARD),
        P(),
        P(None, SHARD),
        P(None, SHARD),
        P(REPLICA, SHARD),
    )
    return jax.shard_map(
        shards,
        mesh=fine,
        in_specs=placed,
        out_specs=(P(REPLICA, SHARD), P(None, SHARD), P(None, SHARD)),
        check_vma=False,
    )
```

time: 390 us -> 111 us (0.28)
  blocking collectives: 248 us -> 46.3 us
  waiting for transfers between devices: 116 us -> 23.6 us
  starting transfers between devices: 0.04 us -> 22.7 us
  between operations: 15.5 us -> 2.22 us
  matrix products: 5.14 us -> 9.81 us
    psum x1 -> x0, blocking collectives: 156 us -> none  [shards(): lax.psum((jnp.sum(weight * weight), jnp.sum(step_sum * step_sum)), ('shar...]
    reduce_scatter x1 -> x0, waiting for transfers between devices: 116 us -> none  [shards(): lax.psum_scatter(lax.dot_general(low_projection, local_grad, (((0,), (0,)...]
    all_gather x3 -> x4, blocking collectives: 91.7 us -> 46.3 us  [pair_sum(): both = lax.all_gather(x, axis, axis=0, tiled=False)]
    all_to_all x0 -> x1, waiting for transfers between devices: none -> 23.6 us  [shards(): lax.all_to_all(jnp.broadcast_to(message[None], (shards_total, 1, 128)), S...]
    all_to_all x0 -> x1, starting transfers between devices: none -> 22.7 us  [shards(): lax.all_to_all(jnp.broadcast_to(message[None], (shards_total, 1, 128)), S...]
    dot_general x2 -> x3, matrix products: 5.14 us -> 9.81 us  [the longest x1 5.22 us: shards(): jnp.dot(projection, normalized, precision=lax.Precision.HIGH, preferred_e...]
  transfers between devices with their start and end apart: 1 -> 1, of which waited for: 1 -> 1; matrix products, arithmetic and copies ran while one was open for 0% -> 1% of each run, Pallas kernels for 0% -> 0%
where the time goes in v1:
time: 111 us
  blocking collectives  46.3 us (42%)
  waiting for transfers between devices  23.6 us (21%)
  starting transfers between devices  22.7 us (20%)
  matrix products  9.81 us (9%)
  local copies, waits for them, and re-layouts  3.79 us (3%)
  other arithmetic  2.59 us (2%)
  between operations  2.22 us (2%)
    all_gather x4, blocking collectives, pair_sum(): both = lax.all_gather(x, axis, axis=0, tiled=False)  46.3 us
    all_to_all x1, waiting for transfers between devices, shards(): lax.all_to_all(jnp.broadcast_to(message[None], (shards_total, 1, 128)), S...  23.6 us
    all_to_all x1, starting transfers between devices, shards(): lax.all_to_all(jnp.broadcast_to(message[None], (shards_total, 1, 128)), S...  22.7 us
    dot_general x1, matrix products, shards(): jnp.dot(projection, normalized, precision=lax.Precision.HIGH, preferred_e...  5.22 us
    dot_general x1, matrix products, shards(): lax.dot_general(low_projection, gradient[0], (((0,), (0,)), ((), ())), pr...  2.47 us
  transfers between devices with their start and end apart: 1, of which 1 were waited for; matrix products, arithmetic and copies ran while one was open for 1% of the time, Pallas kernels for 0%

profile of v1, /device:TPU:1, one launch (start us, length us, event | category | flops | bytes accessed | tf_op | source)
XLA Modules:
  0.0 111.0 jit_solution(5692018902153066786)
XLA Ops:
  0.6 0.0 copy-start
  0.6 1.8 %multiply_reduce_fusion = f32[]{:T(128)} fusion(f32[320,216]{1,0:T(8,128)} %param.9), kind=kLoop, calls=%fused_computation.6 | loop fusion | flops 138239 | bytes 276484 | tf_op jit(solution)/shard_map/reduce_sum | solution.py:32
  2.5 0.0 copy-done
  2.5 2.5 %fusion = f32[128,216]{0,1:T(8,128)S(1)} fusion(bf16[1,5120,216]{1,2,0:T(8,128)(2,1)S(1)} %copy-done, f32[5120,128]{1,0:T(8,128)} %param.6), kind=kOutput, calls=%fused_computation.1 | convolution fusion | flops 283770880 | bytes 4943872 | tf_op jit(solution)/shard_map/dot_general | solution.py:29
  4.9 0.0 copy-start.1
  5.0 0.0 copy-start.2
  5.0 0.7 concatenate.3
  5.7 15.8 %all-gather = f32[256,256]{0,1:T(8,128)S(1)} all-gather(f32[128,256]{0,1:T(8,128)S(1)} %concatenate.3), channel_id=2, replica_groups=mesh['h1'=2,'h0'=2,'y1'=2,'y0'=2,'x1'=2,'x0'=2,'l2'=2,'l1'=2,'l0'=2,'c'=..., dimensions={0}, use_global_device_ids=true | all-gather | bytes 393216 | tf_op jit(solution)/shard_map/all_gather | solution.py:21
  21.5 5.4 %all-gather.1 = f32[256,256]{0,1:T(8,128)S(1)} all-gather(f32[128,256]{0,1:T(8,128)S(1)} %slice_add_fusion.3), channel_id=3, replica_groups=mesh['h1'=2,'h0'=2,'y1'=2,'y0'=2,'x1'=2,'x0'=2,'l2'=2,'l1'=2,'l0'=2,'c'=..., dimensions={0}, use_global_device_ids=true | all-gather | bytes 393216 | tf_op jit(solution)/shard_map/all_gather | solution.py:21
  26.9 0.1 copy.19
  27.0 9.8 %all_gather.21 = f32[2,128,256]{2,1,0:T(8,128)S(1)} all-gather(f32[1,128,256]{2,1,0:T(8,128)S(1)} %copy.19), channel_id=1, replica_groups=mesh['h1'=2,'h0'=2,'y1'=2,'y0'=2,'x1'=2,'x0'=2,'l2'=2,'l1'=2,'l0'=2,'c'=..., dimensions={0}, use_global_device_ids=true | all-gather | bytes 393216 | tf_op jit(solution)/shard_map/all_gather | solution.py:21
  36.8 15.3 %all_gather.22 = f32[2,128,256]{2,1,0:T(8,128)S(1)} all-gather(f32[1,128,256]{2,1,0:T(8,128)S(1)} %slice_add_fusion.1), channel_id=1, replica_groups=mesh['h1'=2,'h0'=2,'y1'=2,'y0'=2,'x1'=2,'x0'=2,'l2'=2,'l1'=2,'l0'=2,'c'=..., dimensions={0}, use_global_device_ids=true | all-gather | bytes 393216 | tf_op jit(solution)/shard_map/all_gather | solution.py:21
  52.1 0.0 copy-done.1
  52.1 0.1 copy.18
  52.2 0.0 copy-done.2
  52.3 0.1 copy.20
  52.4 5.2 %fusion.3 = f32[]{:T(128)} fusion(f32[5120,128]{1,0:T(8,128)} %param.6, f32[128,216]{1,0:T(8,128)S(1)} %get-tuple-element.13, f32[128,216]{1,0:T(8,128)S(1)} %get-tuple-element.12), kind=kOutput, calls=%fused_computation.4 | convolution fusion | flops 851668992 | bytes 2842628 | tf_op jit(solution)/shard_map/dot_general | solution.py:44
  57.6 0.6 fusion.8
  58.3 0.6 broadcast_in_dim.15
  58.9 22.7 %all-to-all-start = ((f32[64,1,128]{2,1,0:T(1,128)}), f32[64,1,128]{2,1,0:T(1,128)S(1)}, u32[]{:S(2)}, u32[]{:S(2)}) async-start(f32[64,1,128]{2,1,0:T(1,128)} %broadcast_in_dim.15), calls=%async_computation | async-start | bytes 65536 | tf_op jit(solution)/shard_map/all_to_all | solution.py:51
  81.6 0.7 copy.22
  82.4 0.7 copy.23
  83.1 23.6 %all-to-all-done = f32[64,1,128]{2,1,0:T(1,128)S(1)} async-done(((f32[64,1,128]{2,1,0:T(1,128)}), f32[64,1,128]{2,1,0:T(1,128)S(1)}, u32[]{:S(2)}, u32[]{:S(2)}) %all-to-all-start) | async-done | bytes 32800 | tf_op jit(solution)/shard_map/all_to_all | solution.py:51
  106.7 0.7 fusion.10
  108.8 2.1 %convolution_multiply_fusion.1 = f32[320,216]{1,0:T(8,128)} fusion(f32[]{:T(128)} %bitcast.5, f32[5120,128]{1,0:T(8,128)} %param.6, s32[]{:T(128)S(6)} %select_n.7, f32[128,216]{1,0:T(8,128)S(1)} %get-tuple-element.13, f32[128,216]{1,0:T(8,128)S(1)} %get-tuple-element.12), kind=kOutput, calls=%fused_computation.5 | convolution fusion | flops 106348032 | bytes 662020 | tf_op jit(solution)/shard_map/dot_general | solution.py:41
  (6 shorter events, 0.1 us)
Async XLA Ops:
  0.6 1.8 %copy-start = (bf16[1,5120,216]{1,2,0:T(8,128)(2,1)S(1)}, bf16[1,5120,216]{1,2,0:T(8,128)(2,1)}, u32[]{:S(2)}) copy-start(bf16[1,5120,216]{1,2,0:T(8,128)(2,1)} %param.5) | copy-start | bytes 6635524
  4.9 47.2 %copy-start.1 = (f32[128,216]{0,1:T(8,128)S(1)}, f32[128,216]{0,1:T(8,128)}, u32[]{:S(2)}) copy-start(f32[128,216]{0,1:T(8,128)} %param.7) | copy-start | bytes 331780
  5.0 47.3 %copy-start.2 = (f32[128,216]{0,1:T(8,128)S(1)}, f32[128,216]{0,1:T(8,128)}, u32[]{:S(2)}) copy-start(f32[128,216]{0,1:T(8,128)} %param.8) | copy-start | bytes 331780
  58.9 47.8 %all-to-all-start = ((f32[64,1,128]{2,1,0:T(1,128)}), f32[64,1,128]{2,1,0:T(1,128)S(1)}, u32[]{:S(2)}, u32[]{:S(2)}) async-start(f32[64,1,128]{2,1,0:T(1,128)} %broadcast_in_dim.15), calls=%async_computation | async-start | bytes 65536 | tf_op jit(solution)/shard_map/all_to_all | solution.py:51

commit v2 on v1

v2 whole, which is shorter than its diff:
```python
import functools

import jax
import jax.numpy as jnp
from jax import lax
from jax.experimental import pallas as pl
from jax.experimental.pallas import tpu as pltpu
from jax.sharding import Mesh, PartitionSpec as P

ADAM_STEP = 10
PLANE = ("y1", "y0", "x1", "x0")
BLOCKS = ("h1", "h0")
SHARD = BLOCKS + PLANE
REPLICA = ("l2", "l1", "l0", "c")
SUBLANES, LANES = 8, 128
MIB = 2**20


def partial_kernel(chunks, gradient, projection, weight, out, grad_v, proj_v, weight_v, sems):
    columns, depth = grad_v.shape
    depth //= chunks
    copies = []
    for i in range(chunks):
        part = pl.ds(i * depth, depth)
        copies.append(
            (
                pltpu.make_async_copy(projection.at[part], proj_v.at[part], sems.at[0, i]),
                pltpu.make_async_copy(gradient.at[:, part], grad_v.at[:, part], sems.at[1, i]),
            )
        )
        for copy in copies[-1]:
            copy.start()
    weight_copy = pltpu.make_async_copy(weight, weight_v, sems.at[2, 0])
    weight_copy.start()
    total = None
    for i in range(chunks):
        for copy in copies[i]:
            copy.wait()
        part = slice(i * depth, (i + 1) * depth)
        term = jnp.dot(
            grad_v[:, part], proj_v[part].astype(jnp.bfloat16), preferred_element_type=jnp.float32
        )
        total = term if total is None else total + term
    out[:columns] = total
    weight_copy.wait()
    weight_sq = jnp.sum(weight_v[...] * weight_v[...])
    out[columns:] = jnp.full((out.shape[0] - columns, out.shape[1]), weight_sq, jnp.float32)


def partial_grad(gradient, projection, weight):
    columns, depth = gradient.shape
    rank = projection.shape[1]
    chunks = 8
    anywhere = pl.BlockSpec(memory_space=pl.ANY)
    return pl.pallas_call(
        functools.partial(partial_kernel, chunks),
        out_shape=jax.ShapeDtypeStruct((columns + SUBLANES, rank), jnp.float32),
        in_specs=[anywhere] * 3,
        out_specs=pl.BlockSpec(memory_space=pltpu.VMEM),
        scratch_shapes=[
            pltpu.VMEM(gradient.shape, gradient.dtype),
            pltpu.VMEM(projection.shape, projection.dtype),
            pltpu.VMEM(weight.shape, weight.dtype),
            pltpu.SemaphoreType.DMA((3, chunks)),
        ],
        compiler_params=pltpu.CompilerParams(vmem_limit_bytes=48 * MIB),
    )(gradient, projection, weight)


def split(x):
    high = x.astype(jnp.bfloat16)
    low = (x - high.astype(jnp.float32)).astype(jnp.bfloat16)
    return high, low


def dot_rows(left, right):
    return lax.dot_general(
        left, right, (((1,), (1,)), ((), ())), preferred_element_type=jnp.float32
    )


def adam_kernel(total, first, second, projection, new_first, new_second, normal, message):
    columns = first.shape[0]
    low_grad = total[:columns]
    moment = 0.9 * first[...] + 0.1 * low_grad
    square = 0.95 * second[...] + 0.05 * low_grad * low_grad
    new_first[...] = moment
    new_second[...] = square
    first_fix = 1.0 - 0.9**ADAM_STEP
    second_fix = 1.0 - 0.95**ADAM_STEP
    normalized = moment / first_fix / (jnp.sqrt(square / second_fix) + 1e-08)
    normal[...] = normalized
    high, low = split(normalized)
    twice = jnp.concatenate([high, high], axis=1)
    depth = 512
    squares = jnp.zeros((SUBLANES, columns), jnp.float32)
    for i in range(projection.shape[0] // depth):
        left, left_low = split(projection[i * depth : (i + 1) * depth])
        step = dot_rows(jnp.concatenate([left, left_low], axis=1), twice) + dot_rows(left, low)
        squares += jnp.sum((step * step).reshape(depth // SUBLANES, SUBLANES, columns), axis=0)
    step_sq = jnp.sum(squares)
    lane = lax.broadcasted_iota(jnp.int32, (1, LANES), 1)
    row = jnp.where(lane == 0, step_sq, total[columns : columns + 1])
    message[...] = jnp.broadcast_to(row[None], message.shape)


def adam_and_norm(total, first, second, projection, partners):
    vmem = pl.BlockSpec(memory_space=pltpu.VMEM)
    shape = jax.ShapeDtypeStruct(first.shape, jnp.float32)
    return pl.pallas_call(
        adam_kernel,
        out_shape=(shape, shape, shape, jax.ShapeDtypeStruct((partners, 1, LANES), jnp.float32)),
        in_specs=[vmem] * 4,
        out_specs=(vmem,) * 4,
        compiler_params=pltpu.CompilerParams(vmem_limit_bytes=24 * MIB),
    )(total, first, second, projection)


def scale_kernel(sums, step, update):
    weight_sq = jnp.broadcast_to(sums[:, 1:2], (1, step.shape[1]))
    step_sq = jnp.broadcast_to(sums[:, :1], (1, step.shape[1]))
    update[...] = step[...] * (jnp.sqrt(weight_sq) / (jnp.sqrt(step_sq) + 1e-06))


def scaled(sums, step):
    vmem = pl.BlockSpec(memory_space=pltpu.VMEM)
    return pl.pallas_call(
        scale_kernel,
        out_shape=jax.ShapeDtypeStruct(step.shape, jnp.float32),
        in_specs=[vmem] * 2,
        out_specs=vmem,
        compiler_params=pltpu.CompilerParams(vmem_limit_bytes=16 * MIB),
    )(sums, step)


def pair_sum(x, axis):
    both = lax.all_gather(x, axis, axis=0, tiled=False)
    return both[0] + both[1]


def shards(gradient, projection, first_moment, second_moment, weight):
    rows_here = weight.shape[0]
    total = pair_sum(partial_grad(jnp.swapaxes(gradient, 1, 2)[0], projection, weight), "c")
    half = total.shape[0] // 2
    total = lax.dynamic_slice_in_dim(total, lax.axis_index("c") * half, half, 0)
    for axis in ("l0", "l1", "l2"):
        total = pair_sum(total, axis)
    total = lax.all_gather(total, "c", axis=0, tiled=True)

    new_first, new_second, normalized, message = adam_and_norm(
        total, first_moment.T, second_moment.T, projection, lax.axis_size(PLANE)
    )
    position = lax.axis_index(REPLICA)
    own_projection = lax.dynamic_slice_in_dim(projection, position * rows_here, rows_here, 0)
    step = jnp.dot(
        own_projection, normalized.T, precision=lax.Precision.HIGHEST, preferred_element_type=jnp.float32
    )
    parts = jnp.sum(lax.all_to_all(message, PLANE, 0, 0), axis=0)
    step, parts = lax.optimization_barrier((step, parts))
    sums = lax.psum(parts, BLOCKS)
    return (scaled(sums, step), new_first.T, new_second.T)


def solution(mesh):
    fine = Mesh(mesh.devices.reshape((2,) * 10), SHARD + REPLICA)
    placed = (
        P(REPLICA, None, SHARD),
        P(),
        P(None, SHARD),
        P(None, SHARD),
        P(REPLICA, SHARD),
    )
    return jax.shard_map(
        shards,
        mesh=fine,
        in_specs=placed,
        out_specs=(P(REPLICA, SHARD), P(None, SHARD), P(None, SHARD)),
        check_vma=False,
    )
```

time: 111 us -> 87.5 us (0.79)
  the two profiles are of different devices: /device:TPU:1 before, /device:TPU:2 now
where the time goes in v2:
time: 87.5 us; the launch traced here: 87.2 us
  blocking collectives  53.8 us (61%)
  starting transfers between devices  15.6 us (18%)
  Pallas kernels  6.5 us (7%)
  waiting for transfers between devices  5.73 us (7%)
  local copies, waits for them, and re-layouts  4.36 us (5%)
    psum x1, blocking collectives, shards(): sums = lax.psum(parts, BLOCKS)  28.6 us
    all_gather x4, blocking collectives, pair_sum(): both = lax.all_gather(x, axis, axis=0, tiled=False)  23.2 us
    all_to_all x1, starting transfers between devices, shards(): parts = jnp.sum(lax.all_to_all(message, PLANE, 0, 0), axis=0)  15.6 us
    all_to_all x1, waiting for transfers between devices, shards(): parts = jnp.sum(lax.all_to_all(message, PLANE, 0, 0), axis=0)  5.73 us
    unnamed x12, local copies, waits for them, and re-layouts  4.34 us
    pallas_call x1, Pallas kernels, partial_grad(): pl.pallas_call(functools.partial(partial_kernel, chunks), out_shape=jax.S...  3.34 us
    pallas_call x1, Pallas kernels, adam_and_norm(): pl.pallas_call(adam_kernel, out_shape=(shape, shape, shape, jax.ShapeDtyp...  2.32 us
    all_gather x1, blocking collectives, shards(): total = lax.all_gather(total, 'c', axis=0, tiled=True)  1.89 us
  transfers between devices with their start and end apart: 1, of which 1 were waited for; matrix products, arithmetic and copies ran while one was open for 1% of the time, Pallas kernels for 0%

profile of v2, /device:TPU:2, one launch (start us, length us, event | category | flops | bytes accessed | tf_op | source)
XLA Modules:
  0.0 87.2 jit_solution(15700434436755190427)
XLA Ops:
  0.6 0.0 copy-start
  0.6 1.7 %copy-done = f32[5120,128]{1,0:T(8,128)S(1)} copy-done((f32[5120,128]{1,0:T(8,128)S(1)}, f32[5120,128]{1,0:T(8,128)}, u32[]{:S(2)}) %copy-start) | copy-done | bytes 2621464
  2.4 0.0 copy-start.2
  2.4 1.6 %copy-done.2 = bf16[1,5120,216]{1,2,0:T(8,128)(2,1)S(1)} copy-done((bf16[1,5120,216]{1,2,0:T(8,128)(2,1)S(1)}, bf16[1,5120,216]{1,2,0:T(8,128)(2,1)}, u32[]{:S(2)}) %copy-start.2) | copy-done | bytes 2211864
  4.0 0.0 copy-start.3
  4.0 1.0 %copy-done.3 = f32[320,216]{1,0:T(8,128)S(1)} copy-done((f32[320,216]{1,0:T(8,128)S(1)}, f32[320,216]{1,0:T(8,128)}, u32[]{:S(2)}) %copy-start.3) | copy-done | bytes 276504
  5.0 0.0 copy-start.1
  5.0 0.0 copy-start.4
  5.0 0.0 copy-start.5
  5.0 3.3 %shard_map.76 = f32[224,128]{1,0:T(8,128)S(1)} custom-call(bf16[216,5120]{1,0:T(8,128)(2,1)S(1)} %bitcast.12, f32[5120,128]{1,0:T(8,128)S(1)} %copy-done, f32[320,216]{1,0:T(8,128)S(1)} %copy-done.3), custom_call_target="tpu_custom_call" | custom-call | tf_op jit(solution)/shard_map/pallas_call | solution.py:55
  8.3 2.0 %all-gather = f32[448,128]{1,0:T(8,128)S(1)} all-gather(f32[224,128]{1,0:T(8,128)S(1)} %shard_map.76), channel_id=2, replica_groups=mesh['h1'=2,'h0'=2,'y1'=2,'y0'=2,'x1'=2,'x0'=2,'l2'=2,'l1'=2,'l0'=2,'c'=..., dimensions={0}, use_global_device_ids=true | all-gather | bytes 344064 | tf_op jit(solution)/shard_map/all_gather | solution.py:137
  10.3 4.9 %all-gather.2 = f32[224,128]{1,0:T(8,128)S(1)} all-gather(f32[112,128]{1,0:T(8,128)S(1)} %dynamic-slice_add_fusion), channel_id=4, replica_groups=mesh['h1'=2,'h0'=2,'y1'=2,'y0'=2,'x1'=2,'x0'=2,'l2'=2,'l1'=2,'l0'=2,'c'=..., dimensions={0}, use_global_device_ids=true | all-gather | bytes 172032 | tf_op jit(solution)/shard_map/all_gather | solution.py:137
  15.2 6.4 %all_gather.24 = f32[2,112,128]{2,1,0:T(8,128)S(1)} all-gather(f32[1,112,128]{2,1,0:T(8,128)S(1)} %fusion.2), channel_id=1, replica_groups=mesh['h1'=2,'h0'=2,'y1'=2,'y0'=2,'x1'=2,'x0'=2,'l2'=2,'l1'=2,'l0'=2,'c'=..., dimensions={0}, use_global_device_ids=true | all-gather | bytes 172032 | tf_op jit(solution)/shard_map/all_gather | solution.py:137
  21.6 10.1 %all_gather.25 = f32[2,112,128]{2,1,0:T(8,128)S(1)} all-gather(f32[1,112,128]{2,1,0:T(8,128)S(1)} %slice_add_fusion.1), channel_id=1, replica_groups=mesh['h1'=2,'h0'=2,'y1'=2,'y0'=2,'x1'=2,'x0'=2,'l2'=2,'l1'=2,'l0'=2,'c'=..., dimensions={0}, use_global_device_ids=true | all-gather | bytes 172032 | tf_op jit(solution)/shard_map/all_gather | solution.py:137
  31.7 1.9 %all-gather.1 = f32[1,224,128]{2,1,0:T(8,128)S(1)} all-gather(f32[1,112,128]{2,1,0:T(8,128)S(1)} %slice_add_fusion), channel_id=3, replica_groups=mesh['h1'=2,'h0'=2,'y1'=2,'y0'=2,'x1'=2,'x0'=2,'l2'=2,'l1'=2,'l0'=2,'c'=..., dimensions={1}, use_global_device_ids=true | all-gather | bytes 172032 | tf_op jit(solution)/shard_map/all_gather | solution.py:148
  33.5 0.0 copy-done.1
  33.5 0.0 copy-done.4
  33.6 0.0 copy-done.5
  33.6 2.3 %shard_map.77 = (f32[216,128]{1,0:T(8,128)}, f32[216,128]{1,0:T(8,128)}, f32[216,128]{1,0:T(8,128)S(1)}, f32[16,1,128]{2,1,0:T(1,128)}) custom-call(f32[224,128]{1,0:T(8,128)S(1)} %bitcast.13, f32[216,128]{1,0:T(8,128)S(1)} %bitcast.14, f32[216,128]{1,0:T(8,128)S(1)} %bitcast.15, f32[5120,128]{1,0:T(8,128)S(1)} %copy-done.1), custom_call_target="tpu_custom_call" | custom-call | tf_op jit(solution)/shard_map/pallas_call | solution.py:110
  35.9 15.6 %all-to-all-start = ((f32[16,1,128]{2,1,0:T(1,128)}), f32[16,1,128]{2,1,0:T(1,128)S(1)}, u32[]{:S(2)}, u32[]{:S(2)}) async-start(f32[16,1,128]{2,1,0:T(1,128)} %get-tuple-element.10), calls=%async_computation | async-start | bytes 16384 | tf_op jit(solution)/shard_map/all_to_all | solution.py:158
  51.5 0.4 fusion.step
  52.0 5.7 %all-to-all-done = f32[16,1,128]{2,1,0:T(1,128)S(1)} async-done(((f32[16,1,128]{2,1,0:T(1,128)}), f32[16,1,128]{2,1,0:T(1,128)S(1)}, u32[]{:S(2)}, u32[]{:S(2)}) %all-to-all-start) | async-done | bytes 8224 | tf_op jit(solution)/shard_map/all_to_all | solution.py:158
  57.7 28.6 %psum.7.sums = f32[1,128]{1,0:T(1,128)S(1)} all-reduce(f32[1,128]{1,0:T(1,128)S(1)} %bitcast.16), channel_id=1, replica_groups=mesh['h1'=2,'h0'=2,'y1'=2,'y0'=2,'x1'=2,'x0'=2,'l2'=2,'l1'=2,'l0'=2,'c'=..., use_global_device_ids=true, to_apply=%region_1.0 | all-reduce | flops 128 | bytes 1024 | tf_op jit(solution)/shard_map/psum | solution.py:160
  86.4 0.8 shard_map.78
  (6 shorter events, 0.1 us)
Async XLA Ops:
  0.6 1.7 %copy-start = (f32[5120,128]{1,0:T(8,128)S(1)}, f32[5120,128]{1,0:T(8,128)}, u32[]{:S(2)}) copy-start(f32[5120,128]{1,0:T(8,128)} %projection.3) | copy-start | bytes 7864324
  2.4 1.6 %copy-start.2 = (bf16[1,5120,216]{1,2,0:T(8,128)(2,1)S(1)}, bf16[1,5120,216]{1,2,0:T(8,128)(2,1)}, u32[]{:S(2)}) copy-start(bf16[1,5120,216]{1,2,0:T(8,128)(2,1)} %param.5) | copy-start | bytes 6635524
  4.0 1.0 %copy-start.3 = (f32[320,216]{1,0:T(8,128)S(1)}, f32[320,216]{1,0:T(8,128)}, u32[]{:S(2)}) copy-start(f32[320,216]{1,0:T(8,128)} %weight.1) | copy-start | bytes 829444
  5.0 28.6 %copy-start.1 = (f32[5120,128]{1,0:T(8,128)S(1)}, f32[5120,128]{1,0:T(8,128)}, u32[]{:S(2)}) copy-start(f32[5120,128]{1,0:T(8,128)} %projection.3) | copy-start | bytes 7864324
  5.0 28.6 %copy-start.4 = (f32[128,216]{0,1:T(8,128)S(1)}, f32[128,216]{0,1:T(8,128)}, u32[]{:S(2)}) copy-start(f32[128,216]{0,1:T(8,128)} %param.7) | copy-start | bytes 331780
  5.0 28.6 %copy-start.5 = (f32[128,216]{0,1:T(8,128)S(1)}, f32[128,216]{0,1:T(8,128)}, u32[]{:S(2)}) copy-start(f32[128,216]{0,1:T(8,128)} %param.8) | copy-start | bytes 331780
  35.9 21.8 %all-to-all-start = ((f32[16,1,128]{2,1,0:T(1,128)}), f32[16,1,128]{2,1,0:T(1,128)S(1)}, u32[]{:S(2)}, u32[]{:S(2)}) async-start(f32[16,1,128]{2,1,0:T(1,128)} %get-tuple-element.10), calls=%async_computation | async-start | bytes 16384 | tf_op jit(solution)/shard_map/all_to_all | solution.py:158

commit v3 on v2

--- a/solution.py
+++ b/solution.py
@@ -50,7 +50,7 @@
 def partial_grad(gradient, projection, weight):
     columns, depth = gradient.shape
     rank = projection.shape[1]
-    chunks = 8
+    chunks = 5
     anywhere = pl.BlockSpec(memory_space=pl.ANY)
     return pl.pallas_call(
         functools.partial(partial_kernel, chunks),
@@ -63,7 +63,7 @@
             pltpu.VMEM(weight.shape, weight.dtype),
             pltpu.SemaphoreType.DMA((3, chunks)),
         ],
-        compiler_params=pltpu.CompilerParams(vmem_limit_bytes=48 * MIB),
+        compiler_params=pltpu.CompilerParams(vmem_limit_bytes=60 * MIB),
     )(gradient, projection, weight)
 
 
@@ -138,6 +138,27 @@
     return both[0] + both[1]
 
 
+def block_permute(x, source, target, mirrored=False):
+    ring = BLOCKS + REPLICA
+    chips, cores = lax.axis_size(REPLICA[:3]), lax.axis_size("c")
+    pairs = []
+    for chip in range(chips):
+        other = chips - 1 - chip if mirrored else chip
+        for core in range(cores):
+            pairs.append(
+                ((source * chips + chip) * cores + core, (target * chips + other) * cores + core)
+            )
+    return lax.ppermute(x, ring, pairs)
+
+
+def blocks_sum(x):
+    total = x
+    for term in (block_permute(x, 2, 0, True), block_permute(x, 1, 0), block_permute(x, 3, 0)):
+        total = total + term
+    spread = [block_permute(total, 0, target) for target in (2, 1, 3)]
+    return jnp.where(lax.axis_index(BLOCKS) == 0, total, spread[0] + spread[1] + spread[2])
+
+
 def shards(gradient, projection, first_moment, second_moment, weight):
     rows_here = weight.shape[0]
     total = pair_sum(partial_grad(jnp.swapaxes(gradient, 1, 2)[0], projection, weight), "c")
@@ -156,9 +177,7 @@
         own_projection, normalized.T, precision=lax.Precision.HIGHEST, preferred_element_type=jnp.float32
     )
     parts = jnp.sum(lax.all_to_all(message, PLANE, 0, 0), axis=0)
-    step, parts = lax.optimization_barrier((step, parts))
-    sums = lax.psum(parts, BLOCKS)
-    return (scaled(sums, step), new_first.T, new_second.T)
+    return (scaled(blocks_sum(parts), step), new_first.T, new_second.T)
 
 
 def solution(mesh):

time: 87.5 us -> 83 us (0.949)
  blocking collectives: 53.8 us -> 25.3 us
  waiting for transfers between devices: 5.73 us -> 22.2 us
  starting transfers between devices: 15.6 us -> 26.8 us
  local copies, waits for them, and re-layouts: 4.36 us -> 0.03 us
    psum x1 -> x0, blocking collectives: 28.6 us -> none  [shards(): sums = lax.psum(parts, BLOCKS)]
    ppermute x0 -> x6, waiting for transfers between devices: none -> 16 us  [block_permute(): return lax.ppermute(x, ring, pairs)]
    ppermute x0 -> x6, starting transfers between devices: none -> 11.2 us  [block_permute(): return lax.ppermute(x, ring, pairs)]
    unnamed x12 -> x6, local copies, waits for them, and re-layouts: 4.34 us -> 0.01 us
  transfers between devices with their start and end apart: 1 -> 7, of which waited for: 1 -> 5; matrix products, arithmetic and copies ran while one was open for 1% -> 1% of each run, Pallas kernels for 0% -> 0%
where the time goes in v3:
time: 83 us; the launch traced here: 82.7 us
  starting transfers between devices  26.8 us (32%)
  blocking collectives  25.3 us (30%)
  waiting for transfers between devices  22.2 us (27%)
  Pallas kernels  6.95 us (8%)
    all_gather x4, blocking collectives, pair_sum(): both = lax.all_gather(x, axis, axis=0, tiled=False)  23.5 us
    ppermute x6, waiting for transfers between devices, block_permute(): return lax.ppermute(x, ring, pairs)  16 us
    all_to_all x1, starting transfers between devices, shards(): parts = jnp.sum(lax.all_to_all(message, PLANE, 0, 0), axis=0)  15.6 us
    ppermute x6, starting transfers between devices, block_permute(): return lax.ppermute(x, ring, pairs)  11.2 us
    all_to_all x1, waiting for transfers between devices, shards(): parts = jnp.sum(lax.all_to_all(message, PLANE, 0, 0), axis=0)  6.18 us
    pallas_call x1, Pallas kernels, partial_grad(): pl.pallas_call(functools.partial(partial_kernel, chunks), out_shape=jax.S...  3.8 us
    pallas_call x1, Pallas kernels, adam_and_norm(): pl.pallas_call(adam_kernel, out_shape=(shape, shape, shape, jax.ShapeDtyp...  2.31 us
    all_gather x1, blocking collectives, shards(): total = lax.all_gather(total, 'c', axis=0, tiled=True)  1.89 us
  transfers between devices with their start and end apart: 7, of which 5 were waited for; matrix products, arithmetic and copies ran while one was open for 1% of the time, Pallas kernels for 0%

profile of v3, /device:TPU:2, one launch (start us, length us, event | category | flops | bytes accessed | tf_op | source)
XLA Modules:
  0.0 82.7 jit_solution(8171792290063183325)
XLA Ops:
  0.6 0.0 copy-start
  0.6 0.0 copy-start.1
  0.7 0.0 copy-start.2
  0.7 3.8 %shard_map.76 = f32[224,128]{1,0:T(8,128)} custom-call(bf16[216,5120]{1,0:T(8,128)(2,1)} %bitcast.16, f32[5120,128]{1,0:T(8,128)} %projection.3, f32[320,216]{1,0:T(8,128)} %weight.1), custom_call_target="tpu_custom_call" | custom-call | tf_op jit(solution)/shard_map/pallas_call | solution.py:55
  4.5 2.2 %all-gather = f32[448,128]{1,0:T(8,128)S(1)} all-gather(f32[224,128]{1,0:T(8,128)} %shard_map.76), channel_id=2, replica_groups=mesh['h1'=2,'h0'=2,'y1'=2,'y0'=2,'x1'=2,'x0'=2,'l2'=2,'l1'=2,'l0'=2,'c'=..., dimensions={0}, use_global_device_ids=true | all-gather | bytes 344064 | tf_op jit(solution)/shard_map/all_gather | solution.py:137
  6.7 4.9 %all-gather.2 = f32[224,128]{1,0:T(8,128)S(1)} all-gather(f32[112,128]{1,0:T(8,128)S(1)} %dynamic-slice_add_fusion), channel_id=4, replica_groups=mesh['h1'=2,'h0'=2,'y1'=2,'y0'=2,'x1'=2,'x0'=2,'l2'=2,'l1'=2,'l0'=2,'c'=..., dimensions={0}, use_global_device_ids=true | all-gather | bytes 172032 | tf_op jit(solution)/shard_map/all_gather | solution.py:137
  11.6 6.4 %all_gather.24 = f32[2,112,128]{2,1,0:T(8,128)S(1)} all-gather(f32[1,112,128]{2,1,0:T(8,128)S(1)} %fusion.2), channel_id=1, replica_groups=mesh['h1'=2,'h0'=2,'y1'=2,'y0'=2,'x1'=2,'x0'=2,'l2'=2,'l1'=2,'l0'=2,'c'=..., dimensions={0}, use_global_device_ids=true | all-gather | bytes 172032 | tf_op jit(solution)/shard_map/all_gather | solution.py:137
  17.9 10.1 %all_gather.25 = f32[2,112,128]{2,1,0:T(8,128)S(1)} all-gather(f32[1,112,128]{2,1,0:T(8,128)S(1)} %slice_add_fusion.1), channel_id=1, replica_groups=mesh['h1'=2,'h0'=2,'y1'=2,'y0'=2,'x1'=2,'x0'=2,'l2'=2,'l1'=2,'l0'=2,'c'=..., dimensions={0}, use_global_device_ids=true | all-gather | bytes 172032 | tf_op jit(solution)/shard_map/all_gather | solution.py:137
  28.0 1.9 %all-gather.1 = f32[1,224,128]{2,1,0:T(8,128)S(1)} all-gather(f32[1,112,128]{2,1,0:T(8,128)S(1)} %slice_add_fusion), channel_id=3, replica_groups=mesh['h1'=2,'h0'=2,'y1'=2,'y0'=2,'x1'=2,'x0'=2,'l2'=2,'l1'=2,'l0'=2,'c'=..., dimensions={1}, use_global_device_ids=true | all-gather | bytes 172032 | tf_op jit(solution)/shard_map/all_gather | solution.py:169
  29.9 0.0 copy-done
  29.9 0.0 copy-done.1
  29.9 0.0 copy-done.2
  29.9 2.3 %shard_map.77 = (f32[216,128]{1,0:T(8,128)}, f32[216,128]{1,0:T(8,128)}, f32[216,128]{1,0:T(8,128)S(1)}, f32[16,1,128]{2,1,0:T(1,128)}) custom-call(f32[224,128]{1,0:T(8,128)S(1)} %bitcast.13, f32[216,128]{1,0:T(8,128)S(1)} %bitcast.14, f32[216,128]{1,0:T(8,128)S(1)} %bitcast.15, f32[5120,128]{1,0:T(8,128)S(1)} %copy-done), custom_call_target="tpu_custom_call" | custom-call | tf_op jit(solution)/shard_map/pallas_call | solution.py:110
  32.2 15.6 %all-to-all-start = ((f32[16,1,128]{2,1,0:T(1,128)}), f32[16,1,128]{2,1,0:T(1,128)S(1)}, u32[]{:S(2)}, u32[]{:S(2)}) async-start(f32[16,1,128]{2,1,0:T(1,128)} %get-tuple-element.7), calls=%async_computation | async-start | bytes 16384 | tf_op jit(solution)/shard_map/all_to_all | solution.py:179
  47.9 6.2 %all-to-all-done = f32[16,1,128]{2,1,0:T(1,128)S(1)} async-done(((f32[16,1,128]{2,1,0:T(1,128)}), f32[16,1,128]{2,1,0:T(1,128)S(1)}, u32[]{:S(2)}, u32[]{:S(2)}) %all-to-all-start) | async-done | bytes 8224 | tf_op jit(solution)/shard_map/all_to_all | solution.py:179
  54.1 1.3 %collective-permute-start.1 = (f32[1,128]{1,0:T(1,128)S(1)}, f32[1,128]{1,0:T(1,128)S(1)}, u32[]{:S(2)}, u32[]{:S(2)}) collective-permute-start(f32[1,128]{1,0:T(1,128)S(1)} %bitcast.17), channel_id=1, source_target_pairs={{256,0},{257,1},{258,2},{259,3},{260,4},{261,5},{262,6},{263,7},{2... | collective-permute-start | bytes 1544 | tf_op jit(solution)/shard_map/ppermute | solution.py:151
  55.4 1.3 %collective-permute-start.2 = (f32[1,128]{1,0:T(1,128)S(1)}, f32[1,128]{1,0:T(1,128)S(1)}, u32[]{:S(2)}, u32[]{:S(2)}) collective-permute-start(f32[1,128]{1,0:T(1,128)S(1)} %bitcast.18), channel_id=1, source_target_pairs={{768,0},{769,1},{770,2},{771,3},{772,4},{773,5},{774,6},{775,7},{7... | collective-permute-start | bytes 1544 | tf_op jit(solution)/shard_map/ppermute | solution.py:151
  56.7 1.3 %collective-permute-start = (f32[1,128]{1,0:T(1,128)S(1)}, f32[1,128]{1,0:T(1,128)S(1)}, u32[]{:S(2)}, u32[]{:S(2)}) collective-permute-start(f32[1,128]{1,0:T(1,128)S(1)} %bitcast.19), channel_id=1, source_target_pairs={{512,14},{513,15},{514,12},{515,13},{516,10},{517,11},{518,8},{519... | collective-permute-start | bytes 1544 | tf_op jit(solution)/shard_map/ppermute | solution.py:151
  58.0 0.5 fusion.step
  58.4 9.8 %collective-permute-done.1 = f32[1,128]{1,0:T(1,128)S(1)} collective-permute-done((f32[1,128]{1,0:T(1,128)S(1)}, f32[1,128]{1,0:T(1,128)S(1)}, u32[]{:S(2)}, u32[]{:S(2)}) %collective-permute-start.1) | collective-permute-done | bytes 544 | tf_op jit(solution)/shard_map/ppermute | solution.py:151
  68.2 2.7 %collective-permute-done.2 = f32[1,128]{1,0:T(1,128)S(1)} collective-permute-done((f32[1,128]{1,0:T(1,128)S(1)}, f32[1,128]{1,0:T(1,128)S(1)}, u32[]{:S(2)}, u32[]{:S(2)}) %collective-permute-start.2) | collective-permute-done | bytes 544 | tf_op jit(solution)/shard_map/ppermute | solution.py:151
  70.9 2.3 %collective-permute-done = f32[1,128]{1,0:T(1,128)S(1)} collective-permute-done((f32[1,128]{1,0:T(1,128)S(1)}, f32[1,128]{1,0:T(1,128)S(1)}, u32[]{:S(2)}, u32[]{:S(2)}) %collective-permute-start) | collective-permute-done | bytes 544 | tf_op jit(solution)/shard_map/ppermute | solution.py:151
  73.2 1.3 %collective-permute-start.5 = (f32[1,128]{1,0:T(1,128)S(1)}, f32[1,128]{1,0:T(1,128)S(1)}, u32[]{:S(2)}, u32[]{:S(2)}) collective-permute-start(f32[1,128]{1,0:T(1,128)S(1)} %add_add_fusion), channel_id=1, source_target_pairs={{0,768},{1,769},{2,770},{3,771},{4,772},{5,773},{6,774},{7,775},{8... | collective-permute-start | bytes 1544 | tf_op jit(solution)/shard_map/ppermute | solution.py:151
  74.5 1.3 %collective-permute-start.4 = (f32[1,128]{1,0:T(1,128)S(1)}, f32[1,128]{1,0:T(1,128)S(1)}, u32[]{:S(2)}, u32[]{:S(2)}) collective-permute-start(f32[1,128]{1,0:T(1,128)S(1)} %add_add_fusion), channel_id=1, source_target_pairs={{0,256},{1,257},{2,258},{3,259},{4,260},{5,261},{6,262},{7,263},{8... | collective-permute-start | bytes 1544 | tf_op jit(solution)/shard_map/ppermute | solution.py:151
  75.8 4.8 %collective-permute-start.3 = (f32[1,128]{1,0:T(1,128)S(1)}, f32[1,128]{1,0:T(1,128)S(1)}, u32[]{:S(2)}, u32[]{:S(2)}) collective-permute-start(f32[1,128]{1,0:T(1,128)S(1)} %add_add_fusion), channel_id=1, source_target_pairs={{0,512},{1,513},{2,514},{3,515},{4,516},{5,517},{6,518},{7,519},{8... | collective-permute-start | bytes 1544 | tf_op jit(solution)/shard_map/ppermute | solution.py:151
  80.6 0.0 collective-permute-done.5
  80.6 0.0 collective-permute-done.4
  80.6 1.2 %collective-permute-done.3 = f32[1,128]{1,0:T(1,128)S(1)} collective-permute-done((f32[1,128]{1,0:T(1,128)S(1)}, f32[1,128]{1,0:T(1,128)S(1)}, u32[]{:S(2)}, u32[]{:S(2)}) %collective-permute-start.3) | collective-permute-done | bytes 544 | tf_op jit(solution)/shard_map/ppermute | solution.py:151
  81.9 0.8 %shard_map.78 = f32[320,216]{1,0:T(8,128)} custom-call(f32[1,128]{1,0:T(1,128)S(1)} %broadcast_select_fusion.sums, f32[320,216]{1,0:T(8,128)S(1)} %fusion.step), custom_call_target="tpu_custom_call" | custom-call | tf_op jit(solution)/shard_map/pallas_call | solution.py:127
  (8 shorter events, 0.1 us)
Async XLA Ops:
  0.6 29.3 %copy-start = (f32[5120,128]{1,0:T(8,128)S(1)}, f32[5120,128]{1,0:T(8,128)}, u32[]{:S(2)}) copy-start(f32[5120,128]{1,0:T(8,128)} %projection.3) | copy-start | bytes 7864324
  0.6 29.3 %copy-start.1 = (f32[128,216]{0,1:T(8,128)S(1)}, f32[128,216]{0,1:T(8,128)}, u32[]{:S(2)}) copy-start(f32[128,216]{0,1:T(8,128)} %param.7) | copy-start | bytes 331780
  0.7 29.2 %copy-start.2 = (f32[128,216]{0,1:T(8,128)S(1)}, f32[128,216]{0,1:T(8,128)}, u32[]{:S(2)}) copy-start(f32[128,216]{0,1:T(8,128)} %param.8) | copy-start | bytes 331780
  32.2 21.8 %all-to-all-start = ((f32[16,1,128]{2,1,0:T(1,128)}), f32[16,1,128]{2,1,0:T(1,128)S(1)}, u32[]{:S(2)}, u32[]{:S(2)}) async-start(f32[16,1,128]{2,1,0:T(1,128)} %get-tuple-element.7), calls=%async_computation | async-start | bytes 16384 | tf_op jit(solution)/shard_map/all_to_all | solution.py:179
  54.1 14.1 %collective-permute-start.1 = (f32[1,128]{1,0:T(1,128)S(1)}, f32[1,128]{1,0:T(1,128)S(1)}, u32[]{:S(2)}, u32[]{:S(2)}) collective-permute-start(f32[1,128]{1,0:T(1,128)S(1)} %bitcast.17), channel_id=1, source_target_pairs={{256,0},{257,1},{258,2},{259,3},{260,4},{261,5},{262,6},{263,7},{2... | collective-permute-start | bytes 1544 | tf_op jit(solution)/shard_map/ppermute | solution.py:151
  55.4 15.5 %collective-permute-start.2 = (f32[1,128]{1,0:T(1,128)S(1)}, f32[1,128]{1,0:T(1,128)S(1)}, u32[]{:S(2)}, u32[]{:S(2)}) collective-permute-start(f32[1,128]{1,0:T(1,128)S(1)} %bitcast.18), channel_id=1, source_target_pairs={{768,0},{769,1},{770,2},{771,3},{772,4},{773,5},{774,6},{775,7},{7... | collective-permute-start | bytes 1544 | tf_op jit(solution)/shard_map/ppermute | solution.py:151
  56.7 16.6 %collective-permute-start = (f32[1,128]{1,0:T(1,128)S(1)}, f32[1,128]{1,0:T(1,128)S(1)}, u32[]{:S(2)}, u32[]{:S(2)}) collective-permute-start(f32[1,128]{1,0:T(1,128)S(1)} %bitcast.19), channel_id=1, source_target_pairs={{512,14},{513,15},{514,12},{515,13},{516,10},{517,11},{518,8},{519... | collective-permute-start | bytes 1544 | tf_op jit(solution)/shard_map/ppermute | solution.py:151
  73.2 7.4 %collective-permute-start.5 = (f32[1,128]{1,0:T(1,128)S(1)}, f32[1,128]{1,0:T(1,128)S(1)}, u32[]{:S(2)}, u32[]{:S(2)}) collective-permute-start(f32[1,128]{1,0:T(1,128)S(1)} %add_add_fusion), channel_id=1, source_target_pairs={{0,768},{1,769},{2,770},{3,771},{4,772},{5,773},{6,774},{7,775},{8... | collective-permute-start | bytes 1544 | tf_op jit(solution)/shard_map/ppermute | solution.py:151
  74.5 6.1 %collective-permute-start.4 = (f32[1,128]{1,0:T(1,128)S(1)}, f32[1,128]{1,0:T(1,128)S(1)}, u32[]{:S(2)}, u32[]{:S(2)}) collective-permute-start(f32[1,128]{1,0:T(1,128)S(1)} %add_add_fusion), channel_id=1, source_target_pairs={{0,256},{1,257},{2,258},{3,259},{4,260},{5,261},{6,262},{7,263},{8... | collective-permute-start | bytes 1544 | tf_op jit(solution)/shard_map/ppermute | solution.py:151
  75.8 6.0 %collective-permute-start.3 = (f32[1,128]{1,0:T(1,128)S(1)}, f32[1,128]{1,0:T(1,128)S(1)}, u32[]{:S(2)}, u32[]{:S(2)}) collective-permute-start(f32[1,128]{1,0:T(1,128)S(1)} %add_add_fusion), channel_id=1, source_target_pairs={{0,512},{1,513},{2,514},{3,515},{4,516},{5,517},{6,518},{7,519},{8... | collective-permute-start | bytes 1544 | tf_op jit(solution)/shard_map/ppermute | solution.py:151

commit v4 on v2

--- a/solution.py
+++ b/solution.py
@@ -50,7 +50,7 @@
 def partial_grad(gradient, projection, weight):
     columns, depth = gradient.shape
     rank = projection.shape[1]
-    chunks = 8
+    chunks = 5
     anywhere = pl.BlockSpec(memory_space=pl.ANY)
     return pl.pallas_call(
         functools.partial(partial_kernel, chunks),
@@ -63,7 +63,7 @@
             pltpu.VMEM(weight.shape, weight.dtype),
             pltpu.SemaphoreType.DMA((3, chunks)),
         ],
-        compiler_params=pltpu.CompilerParams(vmem_limit_bytes=48 * MIB),
+        compiler_params=pltpu.CompilerParams(vmem_limit_bytes=60 * MIB),
     )(gradient, projection, weight)
 
 
@@ -138,6 +138,41 @@
     return both[0] + both[1]
 
 
+def chip_permute(x, moves):
+    cores = lax.axis_size("c")
+    pairs = [(a * cores + c, b * cores + c) for a, b in moves for c in range(cores)]
+    return lax.ppermute(x, BLOCKS + REPLICA, pairs)
+
+
+def run(source, target, count):
+    return [(source + i, target + i) for i in range(count)]
+
+
+def blocks_sum(x):
+    blocks, chips = lax.axis_size(BLOCKS), lax.axis_size(REPLICA[:3])
+    half = chips // 2
+    mirrored = [(2 * chips + i, chips - 1 - i) for i in range(chips)]
+    total = x
+    for moves in (run(chips, 0, chips), mirrored, run(3 * chips, 0, chips)):
+        total = total + chip_permute(x, moves)
+    place = lax.axis_index(BLOCKS + REPLICA[:3])
+    steps = (
+        run(half, chips, half),
+        run(chips, 2 * chips, half) + run(half, blocks * chips - half, half),
+        run(chips, chips + half, half)
+        + run(2 * chips, 2 * chips + half, half)
+        + run(blocks * chips - half, 3 * chips, half),
+    )
+    for moves in steps:
+        starts = {target for _, target in moves if target % half == 0}
+        arrived = chip_permute(total, moves)
+        new = functools.reduce(
+            jnp.logical_or, [(place >= start) & (place < start + half) for start in sorted(starts)]
+        )
+        total = jnp.where(new, arrived, total)
+    return total
+
+
 def shards(gradient, projection, first_moment, second_moment, weight):
     rows_here = weight.shape[0]
     total = pair_sum(partial_grad(jnp.swapaxes(gradient, 1, 2)[0], projection, weight), "c")
@@ -156,9 +191,7 @@
         own_projection, normalized.T, precision=lax.Precision.HIGHEST, preferred_element_type=jnp.float32
     )
     parts = jnp.sum(lax.all_to_all(message, PLANE, 0, 0), axis=0)
-    step, parts = lax.optimization_barrier((step, parts))
-    sums = lax.psum(parts, BLOCKS)
-    return (scaled(sums, step), new_first.T, new_second.T)
+    return (scaled(blocks_sum(parts), step), new_first.T, new_second.T)
 
 
 def solution(mesh):

time: 87.5 us -> 78.8 us (0.901)
  the two profiles are of different devices: /device:TPU:2 before, /device:TPU:640 now
where the time goes in v4:
time: 78.8 us; the launch traced here: 78.5 us
  waiting for transfers between devices  33.8 us (43%)
  blocking collectives  24.1 us (31%)
  starting transfers between devices  12.3 us (16%)
  Pallas kernels  6.96 us (9%)
  between operations  0.91 us (1%)
    ppermute x6, waiting for transfers between devices, chip_permute(): return lax.ppermute(x, BLOCKS + REPLICA, pairs)  26.8 us
    all_gather x4, blocking collectives, pair_sum(): both = lax.all_gather(x, axis, axis=0, tiled=False)  22.2 us
    all_to_all x1, starting transfers between devices, shards(): parts = jnp.sum(lax.all_to_all(message, PLANE, 0, 0), axis=0)  7.04 us
    all_to_all x1, waiting for transfers between devices, shards(): parts = jnp.sum(lax.all_to_all(message, PLANE, 0, 0), axis=0)  7 us
    ppermute x6, starting transfers between devices, chip_permute(): return lax.ppermute(x, BLOCKS + REPLICA, pairs)  5.22 us
    pallas_call x1, Pallas kernels, partial_grad(): pl.pallas_call(functools.partial(partial_kernel, chunks), out_shape=jax.S...  3.8 us
    pallas_call x1, Pallas kernels, adam_and_norm(): pl.pallas_call(adam_kernel, out_shape=(shape, shape, shape, jax.ShapeDtyp...  2.32 us
    all_gather x1, blocking collectives, shards(): total = lax.all_gather(total, 'c', axis=0, tiled=True)  1.89 us
  transfers between devices with their start and end apart: 7, of which 2 were waited for; matrix products, arithmetic and copies ran while one was open for 1% of the time, Pallas kernels for 0%

profile of v4, /device:TPU:640, one launch (start us, length us, event | category | flops | bytes accessed | tf_op | source)
XLA Modules:
  0.0 78.5 jit_solution(14403059708448997286)
XLA Ops:
  0.6 0.0 copy-start
  0.6 0.0 copy-start.1
  0.7 0.0 copy-start.2
  0.7 3.8 %shard_map.76 = f32[224,128]{1,0:T(8,128)} custom-call(bf16[216,5120]{1,0:T(8,128)(2,1)} %bitcast.16, f32[5120,128]{1,0:T(8,128)} %projection.3, f32[320,216]{1,0:T(8,128)} %weight.1), custom_call_target="tpu_custom_call" | custom-call | tf_op jit(solution)/shard_map/pallas_call | solution.py:55
  4.5 2.2 %all-gather = f32[448,128]{1,0:T(8,128)S(1)} all-gather(f32[224,128]{1,0:T(8,128)} %shard_map.76), channel_id=2, replica_groups=mesh['h1'=2,'h0'=2,'y1'=2,'y0'=2,'x1'=2,'x0'=2,'l2'=2,'l1'=2,'l0'=2,'c'=..., dimensions={0}, use_global_device_ids=true | all-gather | bytes 344064 | tf_op jit(solution)/shard_map/all_gather | solution.py:137
  6.7 4.9 %all-gather.2 = f32[224,128]{1,0:T(8,128)S(1)} all-gather(f32[112,128]{1,0:T(8,128)S(1)} %dynamic-slice_add_fusion), channel_id=4, replica_groups=mesh['h1'=2,'h0'=2,'y1'=2,'y0'=2,'x1'=2,'x0'=2,'l2'=2,'l1'=2,'l0'=2,'c'=..., dimensions={0}, use_global_device_ids=true | all-gather | bytes 172032 | tf_op jit(solution)/shard_map/all_gather | solution.py:137
  11.6 6.4 %all_gather.24 = f32[2,112,128]{2,1,0:T(8,128)S(1)} all-gather(f32[1,112,128]{2,1,0:T(8,128)S(1)} %fusion.2), channel_id=1, replica_groups=mesh['h1'=2,'h0'=2,'y1'=2,'y0'=2,'x1'=2,'x0'=2,'l2'=2,'l1'=2,'l0'=2,'c'=..., dimensions={0}, use_global_device_ids=true | all-gather | bytes 172032 | tf_op jit(solution)/shard_map/all_gather | solution.py:137
  17.9 8.8 %all_gather.25 = f32[2,112,128]{2,1,0:T(8,128)S(1)} all-gather(f32[1,112,128]{2,1,0:T(8,128)S(1)} %slice_add_fusion.1), channel_id=1, replica_groups=mesh['h1'=2,'h0'=2,'y1'=2,'y0'=2,'x1'=2,'x0'=2,'l2'=2,'l1'=2,'l0'=2,'c'=..., dimensions={0}, use_global_device_ids=true | all-gather | bytes 172032 | tf_op jit(solution)/shard_map/all_gather | solution.py:137
  26.7 1.9 %all-gather.1 = f32[1,224,128]{2,1,0:T(8,128)S(1)} all-gather(f32[1,112,128]{2,1,0:T(8,128)S(1)} %slice_add_fusion), channel_id=3, replica_groups=mesh['h1'=2,'h0'=2,'y1'=2,'y0'=2,'x1'=2,'x0'=2,'l2'=2,'l1'=2,'l0'=2,'c'=..., dimensions={1}, use_global_device_ids=true | all-gather | bytes 172032 | tf_op jit(solution)/shard_map/all_gather | solution.py:183
  28.6 0.0 copy-done
  28.6 0.0 copy-done.1
  28.6 0.0 copy-done.2
  28.6 2.3 %shard_map.77 = (f32[216,128]{1,0:T(8,128)}, f32[216,128]{1,0:T(8,128)}, f32[216,128]{1,0:T(8,128)S(1)}, f32[16,1,128]{2,1,0:T(1,128)}) custom-call(f32[224,128]{1,0:T(8,128)S(1)} %bitcast.13, f32[216,128]{1,0:T(8,128)S(1)} %bitcast.14, f32[216,128]{1,0:T(8,128)S(1)} %bitcast.15, f32[5120,128]{1,0:T(8,128)S(1)} %copy-done), custom_call_target="tpu_custom_call" | custom-call | tf_op jit(solution)/shard_map/pallas_call | solution.py:110
  30.9 7.0 %all-to-all-start = ((f32[16,1,128]{2,1,0:T(1,128)}), f32[16,1,128]{2,1,0:T(1,128)S(1)}, u32[]{:S(2)}, u32[]{:S(2)}) async-start(f32[16,1,128]{2,1,0:T(1,128)} %get-tuple-element.7), calls=%async_computation | async-start | bytes 16384 | tf_op jit(solution)/shard_map/all_to_all | solution.py:193
  38.0 0.5 fusion.step
  38.5 7.0 %all-to-all-done = f32[16,1,128]{2,1,0:T(1,128)S(1)} async-done(((f32[16,1,128]{2,1,0:T(1,128)}), f32[16,1,128]{2,1,0:T(1,128)S(1)}, u32[]{:S(2)}, u32[]{:S(2)}) %all-to-all-start) | async-done | bytes 8224 | tf_op jit(solution)/shard_map/all_to_all | solution.py:193
  45.5 1.3 %collective-permute-start.1 = (f32[1,128]{1,0:T(1,128)S(1)}, f32[1,128]{1,0:T(1,128)S(1)}, u32[]{:S(2)}, u32[]{:S(2)}) collective-permute-start(f32[1,128]{1,0:T(1,128)S(1)} %bitcast.17), channel_id=1, source_target_pairs={{512,14},{513,15},{514,12},{515,13},{516,10},{517,11},{518,8},{519... | collective-permute-start | bytes 1544 | tf_op jit(solution)/shard_map/ppermute | solution.py:144
  46.8 0.7 collective-permute-start.2
  47.5 0.7 collective-permute-start
  48.1 0.0 collective-permute-done.1
  48.2 0.0 collective-permute-done.2
  48.2 0.0 collective-permute-done
  48.2 0.7 collective-permute-start.3
  48.9 0.0 collective-permute-done.3
  48.9 0.7 collective-permute-start.4
  49.6 0.0 collective-permute-done.4
  49.6 1.3 %collective-permute-start.5 = (f32[1,128]{1,0:T(1,128)S(1)}, f32[1,128]{1,0:T(1,128)S(1)}, u32[]{:S(2)}, u32[]{:S(2)}) collective-permute-start(f32[1,128]{1,0:T(1,128)S(1)} %broadcast_select_fusion.1), channel_id=1, source_target_pairs={{256,264},{257,265},{258,266},{259,267},{260,268},{261,269},{262,2... | collective-permute-start | bytes 1544 | tf_op jit(solution)/shard_map/ppermute | solution.py:144
  50.9 26.8 %collective-permute-done.5 = f32[1,128]{1,0:T(1,128)S(1)} collective-permute-done((f32[1,128]{1,0:T(1,128)S(1)}, f32[1,128]{1,0:T(1,128)S(1)}, u32[]{:S(2)}, u32[]{:S(2)}) %collective-permute-start.5) | collective-permute-done | bytes 544 | tf_op jit(solution)/shard_map/ppermute | solution.py:144
  77.7 0.8 %shard_map.78 = f32[320,216]{1,0:T(8,128)} custom-call(f32[1,128]{1,0:T(1,128)S(1)} %broadcast_select_fusion.2.sums, f32[320,216]{1,0:T(8,128)S(1)} %fusion.step), custom_call_target="tpu_custom_call" | custom-call | tf_op jit(solution)/shard_map/pallas_call | solution.py:127
  (10 shorter events, 0.1 us)
Async XLA Ops:
  0.6 28.0 %copy-start = (f32[5120,128]{1,0:T(8,128)S(1)}, f32[5120,128]{1,0:T(8,128)}, u32[]{:S(2)}) copy-start(f32[5120,128]{1,0:T(8,128)} %projection.3) | copy-start | bytes 7864324
  0.6 28.0 %copy-start.1 = (f32[128,216]{0,1:T(8,128)S(1)}, f32[128,216]{0,1:T(8,128)}, u32[]{:S(2)}) copy-start(f32[128,216]{0,1:T(8,128)} %param.7) | copy-start | bytes 331780
  0.7 28.0 %copy-start.2 = (f32[128,216]{0,1:T(8,128)S(1)}, f32[128,216]{0,1:T(8,128)}, u32[]{:S(2)}) copy-start(f32[128,216]{0,1:T(8,128)} %param.8) | copy-start | bytes 331780
  30.9 14.5 %all-to-all-start = ((f32[16,1,128]{2,1,0:T(1,128)}), f32[16,1,128]{2,1,0:T(1,128)S(1)}, u32[]{:S(2)}, u32[]{:S(2)}) async-start(f32[16,1,128]{2,1,0:T(1,128)} %get-tuple-element.7), calls=%async_computation | async-start | bytes 16384 | tf_op jit(solution)/shard_map/all_to_all | solution.py:193
  45.5 2.6 %collective-permute-start.1 = (f32[1,128]{1,0:T(1,128)S(1)}, f32[1,128]{1,0:T(1,128)S(1)}, u32[]{:S(2)}, u32[]{:S(2)}) collective-permute-start(f32[1,128]{1,0:T(1,128)S(1)} %bitcast.17), channel_id=1, source_target_pairs={{512,14},{513,15},{514,12},{515,13},{516,10},{517,11},{518,8},{519... | collective-permute-start | bytes 1544 | tf_op jit(solution)/shard_map/ppermute | solution.py:144
  46.8 1.4 %collective-permute-start.2 = (f32[1,128]{1,0:T(1,128)S(1)}, f32[1,128]{1,0:T(1,128)S(1)}, u32[]{:S(2)}, u32[]{:S(2)}) collective-permute-start(f32[1,128]{1,0:T(1,128)S(1)} %bitcast.18), channel_id=1, source_target_pairs={{768,0},{769,1},{770,2},{771,3},{772,4},{773,5},{774,6},{775,7},{7... | collective-permute-start | bytes 1544 | tf_op jit(solution)/shard_map/ppermute | solution.py:144
  47.5 0.7 collective-permute-start
  48.2 0.7 collective-permute-start.3
  48.9 0.7 collective-permute-start.4
  49.6 28.1 %collective-permute-start.5 = (f32[1,128]{1,0:T(1,128)S(1)}, f32[1,128]{1,0:T(1,128)S(1)}, u32[]{:S(2)}, u32[]{:S(2)}) collective-permute-start(f32[1,128]{1,0:T(1,128)S(1)} %broadcast_select_fusion.1), channel_id=1, source_target_pairs={{256,264},{257,265},{258,266},{259,267},{260,268},{261,269},{262,2... | collective-permute-start | bytes 1544 | tf_op jit(solution)/shard_map/ppermute | solution.py:144

commit v5 on v4

--- a/solution.py
+++ b/solution.py
@@ -91,12 +91,12 @@
     normalized = moment / first_fix / (jnp.sqrt(square / second_fix) + 1e-08)
     normal[...] = normalized
     high, low = split(normalized)
-    twice = jnp.concatenate([high, high], axis=1)
+    right = jnp.concatenate([high, high, low], axis=1)
     depth = 512
     squares = jnp.zeros((SUBLANES, columns), jnp.float32)
     for i in range(projection.shape[0] // depth):
         left, left_low = split(projection[i * depth : (i + 1) * depth])
-        step = dot_rows(jnp.concatenate([left, left_low], axis=1), twice) + dot_rows(left, low)
+        step = dot_rows(jnp.concatenate([left, left_low, left], axis=1), right)
         squares += jnp.sum((step * step).reshape(depth // SUBLANES, SUBLANES, columns), axis=0)
     step_sq = jnp.sum(squares)
     lane = lax.broadcasted_iota(jnp.int32, (1, LANES), 1)
@@ -160,7 +160,7 @@
         run(half, chips, half),
         run(chips, 2 * chips, half) + run(half, blocks * chips - half, half),
         run(chips, chips + half, half)
-        + run(2 * chips, 2 * chips + half, half)
+        + [(half + i, 3 * chips - 1 - i) for i in range(half)]
         + run(blocks * chips - half, 3 * chips, half),
     )
     for moves in steps:

time: 78.8 us -> 78.9 us (level)
  the two profiles are of different devices: /device:TPU:640 before, /device:TPU:128 now
where the time goes in v5:
time: 78.9 us; the launch traced here: 78.7 us
  blocking collectives  29.6 us (38%)
  waiting for transfers between devices  29.5 us (37%)
  starting transfers between devices  11.2 us (14%)
  Pallas kernels  6.96 us (9%)
  between operations  0.85 us (1%)
    all_gather x4, blocking collectives, pair_sum(): both = lax.all_gather(x, axis, axis=0, tiled=False)  27.7 us
    ppermute x6, waiting for transfers between devices, chip_permute(): return lax.ppermute(x, BLOCKS + REPLICA, pairs)  22.6 us
    ppermute x6, starting transfers between devices, chip_permute(): return lax.ppermute(x, BLOCKS + REPLICA, pairs)  7.71 us
    all_to_all x1, waiting for transfers between devices, shards(): parts = jnp.sum(lax.all_to_all(message, PLANE, 0, 0), axis=0)  6.94 us
    pallas_call x1, Pallas kernels, partial_grad(): pl.pallas_call(functools.partial(partial_kernel, chunks), out_shape=jax.S...  3.8 us
    all_to_all x1, starting transfers between devices, shards(): parts = jnp.sum(lax.all_to_all(message, PLANE, 0, 0), axis=0)  3.47 us
    pallas_call x1, Pallas kernels, adam_and_norm(): pl.pallas_call(adam_kernel, out_shape=(shape, shape, shape, jax.ShapeDtyp...  2.32 us
    all_gather x1, blocking collectives, shards(): total = lax.all_gather(total, 'c', axis=0, tiled=True)  1.88 us
  transfers between devices with their start and end apart: 7, of which 5 were waited for; matrix products, arithmetic and copies ran while one was open for 1% of the time, Pallas kernels for 0%

profile of v5, /device:TPU:128, one launch (start us, length us, event | category | flops | bytes accessed | tf_op | source)
XLA Modules:
  0.0 78.7 jit_solution(17949322821133307172)
XLA Ops:
  0.6 0.0 copy-start
  0.6 0.0 copy-start.1
  0.7 0.0 copy-start.2
  0.7 3.8 %shard_map.76 = f32[224,128]{1,0:T(8,128)} custom-call(bf16[216,5120]{1,0:T(8,128)(2,1)} %bitcast.16, f32[5120,128]{1,0:T(8,128)} %projection.3, f32[320,216]{1,0:T(8,128)} %weight.1), custom_call_target="tpu_custom_call" | custom-call | tf_op jit(solution)/shard_map/pallas_call | solution.py:55
  4.5 2.2 %all-gather = f32[448,128]{1,0:T(8,128)S(1)} all-gather(f32[224,128]{1,0:T(8,128)} %shard_map.76), channel_id=2, replica_groups=mesh['h1'=2,'h0'=2,'y1'=2,'y0'=2,'x1'=2,'x0'=2,'l2'=2,'l1'=2,'l0'=2,'c'=..., dimensions={0}, use_global_device_ids=true | all-gather | bytes 344064 | tf_op jit(solution)/shard_map/all_gather | solution.py:137
  6.7 4.9 %all-gather.2 = f32[224,128]{1,0:T(8,128)S(1)} all-gather(f32[112,128]{1,0:T(8,128)S(1)} %dynamic-slice_add_fusion), channel_id=4, replica_groups=mesh['h1'=2,'h0'=2,'y1'=2,'y0'=2,'x1'=2,'x0'=2,'l2'=2,'l1'=2,'l0'=2,'c'=..., dimensions={0}, use_global_device_ids=true | all-gather | bytes 172032 | tf_op jit(solution)/shard_map/all_gather | solution.py:137
  11.6 6.4 %all_gather.24 = f32[2,112,128]{2,1,0:T(8,128)S(1)} all-gather(f32[1,112,128]{2,1,0:T(8,128)S(1)} %fusion.2), channel_id=1, replica_groups=mesh['h1'=2,'h0'=2,'y1'=2,'y0'=2,'x1'=2,'x0'=2,'l2'=2,'l1'=2,'l0'=2,'c'=..., dimensions={0}, use_global_device_ids=true | all-gather | bytes 172032 | tf_op jit(solution)/shard_map/all_gather | solution.py:137
  17.9 14.3 %all_gather.25 = f32[2,112,128]{2,1,0:T(8,128)S(1)} all-gather(f32[1,112,128]{2,1,0:T(8,128)S(1)} %slice_add_fusion.1), channel_id=1, replica_groups=mesh['h1'=2,'h0'=2,'y1'=2,'y0'=2,'x1'=2,'x0'=2,'l2'=2,'l1'=2,'l0'=2,'c'=..., dimensions={0}, use_global_device_ids=true | all-gather | bytes 172032 | tf_op jit(solution)/shard_map/all_gather | solution.py:137
  32.2 1.9 %all-gather.1 = f32[1,224,128]{2,1,0:T(8,128)S(1)} all-gather(f32[1,112,128]{2,1,0:T(8,128)S(1)} %slice_add_fusion), channel_id=3, replica_groups=mesh['h1'=2,'h0'=2,'y1'=2,'y0'=2,'x1'=2,'x0'=2,'l2'=2,'l1'=2,'l0'=2,'c'=..., dimensions={1}, use_global_device_ids=true | all-gather | bytes 172032 | tf_op jit(solution)/shard_map/all_gather | solution.py:183
  34.1 0.0 copy-done
  34.1 0.0 copy-done.1
  34.1 0.0 copy-done.2
  34.1 2.3 %shard_map.77 = (f32[216,128]{1,0:T(8,128)}, f32[216,128]{1,0:T(8,128)}, f32[216,128]{1,0:T(8,128)S(1)}, f32[16,1,128]{2,1,0:T(1,128)}) custom-call(f32[224,128]{1,0:T(8,128)S(1)} %bitcast.13, f32[216,128]{1,0:T(8,128)S(1)} %bitcast.14, f32[216,128]{1,0:T(8,128)S(1)} %bitcast.15, f32[5120,128]{1,0:T(8,128)S(1)} %copy-done), custom_call_target="tpu_custom_call" | custom-call | tf_op jit(solution)/shard_map/pallas_call | solution.py:110
  36.4 3.5 %all-to-all-start = ((f32[16,1,128]{2,1,0:T(1,128)}), f32[16,1,128]{2,1,0:T(1,128)S(1)}, u32[]{:S(2)}, u32[]{:S(2)}) async-start(f32[16,1,128]{2,1,0:T(1,128)} %get-tuple-element.7), calls=%async_computation | async-start | bytes 16384 | tf_op jit(solution)/shard_map/all_to_all | solution.py:193
  39.9 0.5 fusion.step
  40.4 6.9 %all-to-all-done = f32[16,1,128]{2,1,0:T(1,128)S(1)} async-done(((f32[16,1,128]{2,1,0:T(1,128)}), f32[16,1,128]{2,1,0:T(1,128)S(1)}, u32[]{:S(2)}, u32[]{:S(2)}) %all-to-all-start) | async-done | bytes 8224 | tf_op jit(solution)/shard_map/all_to_all | solution.py:193
  47.4 1.3 %collective-permute-start.1 = (f32[1,128]{1,0:T(1,128)S(1)}, f32[1,128]{1,0:T(1,128)S(1)}, u32[]{:S(2)}, u32[]{:S(2)}) collective-permute-start(f32[1,128]{1,0:T(1,128)S(1)} %bitcast.17), channel_id=1, source_target_pairs={{512,14},{513,15},{514,12},{515,13},{516,10},{517,11},{518,8},{519... | collective-permute-start | bytes 1544 | tf_op jit(solution)/shard_map/ppermute | solution.py:144
  48.7 1.3 %collective-permute-start.2 = (f32[1,128]{1,0:T(1,128)S(1)}, f32[1,128]{1,0:T(1,128)S(1)}, u32[]{:S(2)}, u32[]{:S(2)}) collective-permute-start(f32[1,128]{1,0:T(1,128)S(1)} %bitcast.18), channel_id=1, source_target_pairs={{768,0},{769,1},{770,2},{771,3},{772,4},{773,5},{774,6},{775,7},{7... | collective-permute-start | bytes 1544 | tf_op jit(solution)/shard_map/ppermute | solution.py:144
  50.0 1.3 %collective-permute-start = (f32[1,128]{1,0:T(1,128)S(1)}, f32[1,128]{1,0:T(1,128)S(1)}, u32[]{:S(2)}, u32[]{:S(2)}) collective-permute-start(f32[1,128]{1,0:T(1,128)S(1)} %bitcast.19), channel_id=1, source_target_pairs={{256,0},{257,1},{258,2},{259,3},{260,4},{261,5},{262,6},{263,7},{2... | collective-permute-start | bytes 1544 | tf_op jit(solution)/shard_map/ppermute | solution.py:144
  51.3 18.8 %collective-permute-done.1 = f32[1,128]{1,0:T(1,128)S(1)} collective-permute-done((f32[1,128]{1,0:T(1,128)S(1)}, f32[1,128]{1,0:T(1,128)S(1)}, u32[]{:S(2)}, u32[]{:S(2)}) %collective-permute-start.1) | collective-permute-done | bytes 544 | tf_op jit(solution)/shard_map/ppermute | solution.py:144
  70.1 0.0 collective-permute-done.2
  70.1 0.0 collective-permute-done
  70.1 1.3 %collective-permute-start.3 = (f32[1,128]{1,0:T(1,128)S(1)}, f32[1,128]{1,0:T(1,128)S(1)}, u32[]{:S(2)}, u32[]{:S(2)}) collective-permute-start(f32[1,128]{1,0:T(1,128)S(1)} %add_add_fusion), channel_id=1, source_target_pairs={{8,256},{9,257},{10,258},{11,259},{12,260},{13,261},{14,262},{15,2... | collective-permute-start | bytes 1544 | tf_op jit(solution)/shard_map/ppermute | solution.py:144
  71.4 1.3 %collective-permute-done.3 = f32[1,128]{1,0:T(1,128)S(1)} collective-permute-done((f32[1,128]{1,0:T(1,128)S(1)}, f32[1,128]{1,0:T(1,128)S(1)}, u32[]{:S(2)}, u32[]{:S(2)}) %collective-permute-start.3) | collective-permute-done | bytes 544 | tf_op jit(solution)/shard_map/ppermute | solution.py:144
  72.7 1.3 %collective-permute-start.4 = (f32[1,128]{1,0:T(1,128)S(1)}, f32[1,128]{1,0:T(1,128)S(1)}, u32[]{:S(2)}, u32[]{:S(2)}) collective-permute-start(f32[1,128]{1,0:T(1,128)S(1)} %broadcast_select_fusion), channel_id=1, source_target_pairs={{256,512},{257,513},{258,514},{259,515},{260,516},{261,517},{262,5... | collective-permute-start | bytes 1544 | tf_op jit(solution)/shard_map/ppermute | solution.py:144
  74.0 1.3 %collective-permute-done.4 = f32[1,128]{1,0:T(1,128)S(1)} collective-permute-done((f32[1,128]{1,0:T(1,128)S(1)}, f32[1,128]{1,0:T(1,128)S(1)}, u32[]{:S(2)}, u32[]{:S(2)}) %collective-permute-start.4) | collective-permute-done | bytes 544 | tf_op jit(solution)/shard_map/ppermute | solution.py:144
  75.3 1.3 %collective-permute-start.5 = (f32[1,128]{1,0:T(1,128)S(1)}, f32[1,128]{1,0:T(1,128)S(1)}, u32[]{:S(2)}, u32[]{:S(2)}) collective-permute-start(f32[1,128]{1,0:T(1,128)S(1)} %broadcast_select_fusion.1), channel_id=1, source_target_pairs={{256,264},{257,265},{258,266},{259,267},{260,268},{261,269},{262,2... | collective-permute-start | bytes 1544 | tf_op jit(solution)/shard_map/ppermute | solution.py:144
  76.6 1.3 %collective-permute-done.5 = f32[1,128]{1,0:T(1,128)S(1)} collective-permute-done((f32[1,128]{1,0:T(1,128)S(1)}, f32[1,128]{1,0:T(1,128)S(1)}, u32[]{:S(2)}, u32[]{:S(2)}) %collective-permute-start.5) | collective-permute-done | bytes 544 | tf_op jit(solution)/shard_map/ppermute | solution.py:144
  77.8 0.8 %shard_map.78 = f32[320,216]{1,0:T(8,128)} custom-call(f32[1,128]{1,0:T(1,128)S(1)} %broadcast_select_fusion.2.sums, f32[320,216]{1,0:T(8,128)S(1)} %fusion.step), custom_call_target="tpu_custom_call" | custom-call | tf_op jit(solution)/shard_map/pallas_call | solution.py:127
  (10 shorter events, 0.1 us)
Async XLA Ops:
  0.6 33.5 %copy-start = (f32[5120,128]{1,0:T(8,128)S(1)}, f32[5120,128]{1,0:T(8,128)}, u32[]{:S(2)}) copy-start(f32[5120,128]{1,0:T(8,128)} %projection.3) | copy-start | bytes 7864324
  0.6 33.5 %copy-start.1 = (f32[128,216]{0,1:T(8,128)S(1)}, f32[128,216]{0,1:T(8,128)}, u32[]{:S(2)}) copy-start(f32[128,216]{0,1:T(8,128)} %param.7) | copy-start | bytes 331780
  0.7 33.5 %copy-start.2 = (f32[128,216]{0,1:T(8,128)S(1)}, f32[128,216]{0,1:T(8,128)}, u32[]{:S(2)}) copy-start(f32[128,216]{0,1:T(8,128)} %param.8) | copy-start | bytes 331780
  36.4 10.9 %all-to-all-start = ((f32[16,1,128]{2,1,0:T(1,128)}), f32[16,1,128]{2,1,0:T(1,128)S(1)}, u32[]{:S(2)}, u32[]{:S(2)}) async-start(f32[16,1,128]{2,1,0:T(1,128)} %get-tuple-element.7), calls=%async_computation | async-start | bytes 16384 | tf_op jit(solution)/shard_map/all_to_all | solution.py:193
  47.4 22.7 %collective-permute-start.1 = (f32[1,128]{1,0:T(1,128)S(1)}, f32[1,128]{1,0:T(1,128)S(1)}, u32[]{:S(2)}, u32[]{:S(2)}) collective-permute-start(f32[1,128]{1,0:T(1,128)S(1)} %bitcast.17), channel_id=1, source_target_pairs={{512,14},{513,15},{514,12},{515,13},{516,10},{517,11},{518,8},{519... | collective-permute-start | bytes 1544 | tf_op jit(solution)/shard_map/ppermute | solution.py:144
  48.7 21.4 %collective-permute-start.2 = (f32[1,128]{1,0:T(1,128)S(1)}, f32[1,128]{1,0:T(1,128)S(1)}, u32[]{:S(2)}, u32[]{:S(2)}) collective-permute-start(f32[1,128]{1,0:T(1,128)S(1)} %bitcast.18), channel_id=1, source_target_pairs={{768,0},{769,1},{770,2},{771,3},{772,4},{773,5},{774,6},{775,7},{7... | collective-permute-start | bytes 1544 | tf_op jit(solution)/shard_map/ppermute | solution.py:144
  50.0 20.1 %collective-permute-start = (f32[1,128]{1,0:T(1,128)S(1)}, f32[1,128]{1,0:T(1,128)S(1)}, u32[]{:S(2)}, u32[]{:S(2)}) collective-permute-start(f32[1,128]{1,0:T(1,128)S(1)} %bitcast.19), channel_id=1, source_target_pairs={{256,0},{257,1},{258,2},{259,3},{260,4},{261,5},{262,6},{263,7},{2... | collective-permute-start | bytes 1544 | tf_op jit(solution)/shard_map/ppermute | solution.py:144
  70.1 2.6 %collective-permute-start.3 = (f32[1,128]{1,0:T(1,128)S(1)}, f32[1,128]{1,0:T(1,128)S(1)}, u32[]{:S(2)}, u32[]{:S(2)}) collective-permute-start(f32[1,128]{1,0:T(1,128)S(1)} %add_add_fusion), channel_id=1, source_target_pairs={{8,256},{9,257},{10,258},{11,259},{12,260},{13,261},{14,262},{15,2... | collective-permute-start | bytes 1544 | tf_op jit(solution)/shard_map/ppermute | solution.py:144
  72.7 2.6 %collective-permute-start.4 = (f32[1,128]{1,0:T(1,128)S(1)}, f32[1,128]{1,0:T(1,128)S(1)}, u32[]{:S(2)}, u32[]{:S(2)}) collective-permute-start(f32[1,128]{1,0:T(1,128)S(1)} %broadcast_select_fusion), channel_id=1, source_target_pairs={{256,512},{257,513},{258,514},{259,515},{260,516},{261,517},{262,5... | collective-permute-start | bytes 1544 | tf_op jit(solution)/shard_map/ppermute | solution.py:144
  75.3 2.6 %collective-permute-start.5 = (f32[1,128]{1,0:T(1,128)S(1)}, f32[1,128]{1,0:T(1,128)S(1)}, u32[]{:S(2)}, u32[]{:S(2)}) collective-permute-start(f32[1,128]{1,0:T(1,128)S(1)} %broadcast_select_fusion.1), channel_id=1, source_target_pairs={{256,264},{257,265},{258,266},{259,267},{260,268},{261,269},{262,2... | collective-permute-start | bytes 1544 | tf_op jit(solution)/shard_map/ppermute | solution.py:144

commit v6 on v5

--- a/solution.py
+++ b/solution.py
@@ -138,6 +138,13 @@
     return both[0] + both[1]
 
 
+SPREAD = (
+    ((7, 8), (6, 9), (5, 10), (4, 11)),
+    ((8, 16), (9, 17), (10, 18), (11, 19), (7, 29), (6, 30), (5, 31), (4, 28)),
+    ((8, 12), (9, 13), (10, 14), (11, 15), (16, 20), (17, 21), (7, 22), (6, 23), (31, 24), (28, 25), (30, 26), (29, 27)),
+)
+
+
 def chip_permute(x, moves):
     cores = lax.axis_size("c")
     pairs = [(a * cores + c, b * cores + c) for a, b in moves for c in range(cores)]
@@ -149,25 +156,18 @@
 
 
 def blocks_sum(x):
-    blocks, chips = lax.axis_size(BLOCKS), lax.axis_size(REPLICA[:3])
+    chips = lax.axis_size(REPLICA[:3])
     half = chips // 2
     mirrored = [(2 * chips + i, chips - 1 - i) for i in range(chips)]
     total = x
     for moves in (run(chips, 0, chips), mirrored, run(3 * chips, 0, chips)):
         total = total + chip_permute(x, moves)
     place = lax.axis_index(BLOCKS + REPLICA[:3])
-    steps = (
-        run(half, chips, half),
-        run(chips, 2 * chips, half) + run(half, blocks * chips - half, half),
-        run(chips, chips + half, half)
-        + [(half + i, 3 * chips - 1 - i) for i in range(half)]
-        + run(blocks * chips - half, 3 * chips, half),
-    )
-    for moves in steps:
-        starts = {target for _, target in moves if target % half == 0}
+    for moves in SPREAD:
+        targets = {target - target % half for _, target in moves}
         arrived = chip_permute(total, moves)
         new = functools.reduce(
-            jnp.logical_or, [(place >= start) & (place < start + half) for start in sorted(starts)]
+            jnp.logical_or, [(place >= start) & (place < start + half) for start in sorted(targets)]
         )
         total = jnp.where(new, arrived, total)
     return total

time: 78.9 us -> 77.1 us (0.977)
  waiting for transfers between devices: 29.5 us -> 28.3 us
    ppermute x6, waiting for transfers between devices: 22.6 us -> 21.3 us  [chip_permute(): return lax.ppermute(x, BLOCKS + REPLICA, pairs)]
  transfers between devices with their start and end apart: 7 -> 7, of which waited for: 5 -> 4; matrix products, arithmetic and copies ran while one was open for 1% -> 1% of each run, Pallas kernels for 0% -> 0%
where the time goes in v6:
time: 77.1 us; the launch traced here: 76.8 us
  blocking collectives  29.6 us (38%)
  waiting for transfers between devices  28.3 us (37%)
  starting transfers between devices  10.6 us (14%)
  Pallas kernels  6.96 us (9%)
  between operations  0.87 us (1%)
    all_gather x4, blocking collectives, pair_sum(): both = lax.all_gather(x, axis, axis=0, tiled=False)  27.7 us
    ppermute x6, waiting for transfers between devices, chip_permute(): return lax.ppermute(x, BLOCKS + REPLICA, pairs)  21.3 us
    ppermute x6, starting transfers between devices, chip_permute(): return lax.ppermute(x, BLOCKS + REPLICA, pairs)  7.08 us
    all_to_all x1, waiting for transfers between devices, shards(): parts = jnp.sum(lax.all_to_all(message, PLANE, 0, 0), axis=0)  6.94 us
    pallas_call x1, Pallas kernels, partial_grad(): pl.pallas_call(functools.partial(partial_kernel, chunks), out_shape=jax.S...  3.8 us
    all_to_all x1, starting transfers between devices, shards(): parts = jnp.sum(lax.all_to_all(message, PLANE, 0, 0), axis=0)  3.47 us
    pallas_call x1, Pallas kernels, adam_and_norm(): pl.pallas_call(adam_kernel, out_shape=(shape, shape, shape, jax.ShapeDtyp...  2.32 us
    all_gather x1, blocking collectives, shards(): total = lax.all_gather(total, 'c', axis=0, tiled=True)  1.88 us
  transfers between devices with their start and end apart: 7, of which 4 were waited for; matrix products, arithmetic and copies ran while one was open for 1% of the time, Pallas kernels for 0%

profile of v6, /device:TPU:128, one launch (start us, length us, event | category | flops | bytes accessed | tf_op | source)
XLA Modules:
  0.0 76.8 jit_solution(18271386460956709421)
XLA Ops:
  0.6 0.0 copy-start
  0.6 0.0 copy-start.1
  0.7 0.0 copy-start.2
  0.7 3.8 %shard_map.76 = f32[224,128]{1,0:T(8,128)} custom-call(bf16[216,5120]{1,0:T(8,128)(2,1)} %bitcast.16, f32[5120,128]{1,0:T(8,128)} %projection.3, f32[320,216]{1,0:T(8,128)} %weight.1), custom_call_target="tpu_custom_call" | custom-call | tf_op jit(solution)/shard_map/pallas_call | solution.py:55
  4.5 2.2 %all-gather = f32[448,128]{1,0:T(8,128)S(1)} all-gather(f32[224,128]{1,0:T(8,128)} %shard_map.76), channel_id=2, replica_groups=mesh['h1'=2,'h0'=2,'y1'=2,'y0'=2,'x1'=2,'x0'=2,'l2'=2,'l1'=2,'l0'=2,'c'=..., dimensions={0}, use_global_device_ids=true | all-gather | bytes 344064 | tf_op jit(solution)/shard_map/all_gather | solution.py:137
  6.7 4.9 %all-gather.2 = f32[224,128]{1,0:T(8,128)S(1)} all-gather(f32[112,128]{1,0:T(8,128)S(1)} %dynamic-slice_add_fusion), channel_id=4, replica_groups=mesh['h1'=2,'h0'=2,'y1'=2,'y0'=2,'x1'=2,'x0'=2,'l2'=2,'l1'=2,'l0'=2,'c'=..., dimensions={0}, use_global_device_ids=true | all-gather | bytes 172032 | tf_op jit(solution)/shard_map/all_gather | solution.py:137
  11.6 6.4 %all_gather.24 = f32[2,112,128]{2,1,0:T(8,128)S(1)} all-gather(f32[1,112,128]{2,1,0:T(8,128)S(1)} %fusion.2), channel_id=1, replica_groups=mesh['h1'=2,'h0'=2,'y1'=2,'y0'=2,'x1'=2,'x0'=2,'l2'=2,'l1'=2,'l0'=2,'c'=..., dimensions={0}, use_global_device_ids=true | all-gather | bytes 172032 | tf_op jit(solution)/shard_map/all_gather | solution.py:137
  17.9 14.3 %all_gather.25 = f32[2,112,128]{2,1,0:T(8,128)S(1)} all-gather(f32[1,112,128]{2,1,0:T(8,128)S(1)} %slice_add_fusion.1), channel_id=1, replica_groups=mesh['h1'=2,'h0'=2,'y1'=2,'y0'=2,'x1'=2,'x0'=2,'l2'=2,'l1'=2,'l0'=2,'c'=..., dimensions={0}, use_global_device_ids=true | all-gather | bytes 172032 | tf_op jit(solution)/shard_map/all_gather | solution.py:137
  32.2 1.9 %all-gather.1 = f32[1,224,128]{2,1,0:T(8,128)S(1)} all-gather(f32[1,112,128]{2,1,0:T(8,128)S(1)} %slice_add_fusion), channel_id=3, replica_groups=mesh['h1'=2,'h0'=2,'y1'=2,'y0'=2,'x1'=2,'x0'=2,'l2'=2,'l1'=2,'l0'=2,'c'=..., dimensions={1}, use_global_device_ids=true | all-gather | bytes 172032 | tf_op jit(solution)/shard_map/all_gather | solution.py:183
  34.1 0.0 copy-done
  34.1 0.0 copy-done.1
  34.1 0.0 copy-done.2
  34.1 2.3 %shard_map.77 = (f32[216,128]{1,0:T(8,128)}, f32[216,128]{1,0:T(8,128)}, f32[216,128]{1,0:T(8,128)S(1)}, f32[16,1,128]{2,1,0:T(1,128)}) custom-call(f32[224,128]{1,0:T(8,128)S(1)} %bitcast.13, f32[216,128]{1,0:T(8,128)S(1)} %bitcast.14, f32[216,128]{1,0:T(8,128)S(1)} %bitcast.15, f32[5120,128]{1,0:T(8,128)S(1)} %copy-done), custom_call_target="tpu_custom_call" | custom-call | tf_op jit(solution)/shard_map/pallas_call | solution.py:110
  36.4 3.5 %all-to-all-start = ((f32[16,1,128]{2,1,0:T(1,128)}), f32[16,1,128]{2,1,0:T(1,128)S(1)}, u32[]{:S(2)}, u32[]{:S(2)}) async-start(f32[16,1,128]{2,1,0:T(1,128)} %get-tuple-element.7), calls=%async_computation | async-start | bytes 16384 | tf_op jit(solution)/shard_map/all_to_all | solution.py:193
  39.9 0.5 fusion.step
  40.4 6.9 %all-to-all-done = f32[16,1,128]{2,1,0:T(1,128)S(1)} async-done(((f32[16,1,128]{2,1,0:T(1,128)}), f32[16,1,128]{2,1,0:T(1,128)S(1)}, u32[]{:S(2)}, u32[]{:S(2)}) %all-to-all-start) | async-done | bytes 8224 | tf_op jit(solution)/shard_map/all_to_all | solution.py:193
  47.4 1.3 %collective-permute-start.1 = (f32[1,128]{1,0:T(1,128)S(1)}, f32[1,128]{1,0:T(1,128)S(1)}, u32[]{:S(2)}, u32[]{:S(2)}) collective-permute-start(f32[1,128]{1,0:T(1,128)S(1)} %bitcast.17), channel_id=1, source_target_pairs={{512,14},{513,15},{514,12},{515,13},{516,10},{517,11},{518,8},{519... | collective-permute-start | bytes 1544 | tf_op jit(solution)/shard_map/ppermute | solution.py:151
  48.7 1.3 %collective-permute-start.2 = (f32[1,128]{1,0:T(1,128)S(1)}, f32[1,128]{1,0:T(1,128)S(1)}, u32[]{:S(2)}, u32[]{:S(2)}) collective-permute-start(f32[1,128]{1,0:T(1,128)S(1)} %bitcast.18), channel_id=1, source_target_pairs={{768,0},{769,1},{770,2},{771,3},{772,4},{773,5},{774,6},{775,7},{7... | collective-permute-start | bytes 1544 | tf_op jit(solution)/shard_map/ppermute | solution.py:151
  50.0 1.3 %collective-permute-start = (f32[1,128]{1,0:T(1,128)S(1)}, f32[1,128]{1,0:T(1,128)S(1)}, u32[]{:S(2)}, u32[]{:S(2)}) collective-permute-start(f32[1,128]{1,0:T(1,128)S(1)} %bitcast.19), channel_id=1, source_target_pairs={{256,0},{257,1},{258,2},{259,3},{260,4},{261,5},{262,6},{263,7},{2... | collective-permute-start | bytes 1544 | tf_op jit(solution)/shard_map/ppermute | solution.py:151
  51.3 18.8 %collective-permute-done.1 = f32[1,128]{1,0:T(1,128)S(1)} collective-permute-done((f32[1,128]{1,0:T(1,128)S(1)}, f32[1,128]{1,0:T(1,128)S(1)}, u32[]{:S(2)}, u32[]{:S(2)}) %collective-permute-start.1) | collective-permute-done | bytes 544 | tf_op jit(solution)/shard_map/ppermute | solution.py:151
  70.1 0.0 collective-permute-done.2
  70.1 0.0 collective-permute-done
  70.1 1.3 %collective-permute-start.3 = (f32[1,128]{1,0:T(1,128)S(1)}, f32[1,128]{1,0:T(1,128)S(1)}, u32[]{:S(2)}, u32[]{:S(2)}) collective-permute-start(f32[1,128]{1,0:T(1,128)S(1)} %add_add_fusion), channel_id=1, source_target_pairs={{14,256},{15,257},{12,258},{13,259},{10,260},{11,261},{8,262},{9,2... | collective-permute-start | bytes 1544 | tf_op jit(solution)/shard_map/ppermute | solution.py:151
  71.4 1.3 %collective-permute-done.3 = f32[1,128]{1,0:T(1,128)S(1)} collective-permute-done((f32[1,128]{1,0:T(1,128)S(1)}, f32[1,128]{1,0:T(1,128)S(1)}, u32[]{:S(2)}, u32[]{:S(2)}) %collective-permute-start.3) | collective-permute-done | bytes 544 | tf_op jit(solution)/shard_map/ppermute | solution.py:151
  72.7 1.3 %collective-permute-start.4 = (f32[1,128]{1,0:T(1,128)S(1)}, f32[1,128]{1,0:T(1,128)S(1)}, u32[]{:S(2)}, u32[]{:S(2)}) collective-permute-start(f32[1,128]{1,0:T(1,128)S(1)} %broadcast_select_fusion), channel_id=1, source_target_pairs={{256,512},{257,513},{258,514},{259,515},{260,516},{261,517},{262,5... | collective-permute-start | bytes 1544 | tf_op jit(solution)/shard_map/ppermute | solution.py:151
  74.0 1.3 %collective-permute-done.4 = f32[1,128]{1,0:T(1,128)S(1)} collective-permute-done((f32[1,128]{1,0:T(1,128)S(1)}, f32[1,128]{1,0:T(1,128)S(1)}, u32[]{:S(2)}, u32[]{:S(2)}) %collective-permute-start.4) | collective-permute-done | bytes 544 | tf_op jit(solution)/shard_map/ppermute | solution.py:151
  75.3 0.6 collective-permute-start.5
  75.9 0.0 collective-permute-done.5
  76.0 0.8 %shard_map.78 = f32[320,216]{1,0:T(8,128)} custom-call(f32[1,128]{1,0:T(1,128)S(1)} %broadcast_select_fusion.2.sums, f32[320,216]{1,0:T(8,128)S(1)} %fusion.step), custom_call_target="tpu_custom_call" | custom-call | tf_op jit(solution)/shard_map/pallas_call | solution.py:127
  (10 shorter events, 0.1 us)
Async XLA Ops:
  0.6 33.5 %copy-start = (f32[5120,128]{1,0:T(8,128)S(1)}, f32[5120,128]{1,0:T(8,128)}, u32[]{:S(2)}) copy-start(f32[5120,128]{1,0:T(8,128)} %projection.3) | copy-start | bytes 7864324
  0.6 33.5 %copy-start.1 = (f32[128,216]{0,1:T(8,128)S(1)}, f32[128,216]{0,1:T(8,128)}, u32[]{:S(2)}) copy-start(f32[128,216]{0,1:T(8,128)} %param.7) | copy-start | bytes 331780
  0.7 33.5 %copy-start.2 = (f32[128,216]{0,1:T(8,128)S(1)}, f32[128,216]{0,1:T(8,128)}, u32[]{:S(2)}) copy-start(f32[128,216]{0,1:T(8,128)} %param.8) | copy-start | bytes 331780
  36.4 10.9 %all-to-all-start = ((f32[16,1,128]{2,1,0:T(1,128)}), f32[16,1,128]{2,1,0:T(1,128)S(1)}, u32[]{:S(2)}, u32[]{:S(2)}) async-start(f32[16,1,128]{2,1,0:T(1,128)} %get-tuple-element.7), calls=%async_computation | async-start | bytes 16384 | tf_op jit(solution)/shard_map/all_to_all | solution.py:193
  47.4 22.7 %collective-permute-start.1 = (f32[1,128]{1,0:T(1,128)S(1)}, f32[1,128]{1,0:T(1,128)S(1)}, u32[]{:S(2)}, u32[]{:S(2)}) collective-permute-start(f32[1,128]{1,0:T(1,128)S(1)} %bitcast.17), channel_id=1, source_target_pairs={{512,14},{513,15},{514,12},{515,13},{516,10},{517,11},{518,8},{519... | collective-permute-start | bytes 1544 | tf_op jit(solution)/shard_map/ppermute | solution.py:151
  48.7 21.4 %collective-permute-start.2 = (f32[1,128]{1,0:T(1,128)S(1)}, f32[1,128]{1,0:T(1,128)S(1)}, u32[]{:S(2)}, u32[]{:S(2)}) collective-permute-start(f32[1,128]{1,0:T(1,128)S(1)} %bitcast.18), channel_id=1, source_target_pairs={{768,0},{769,1},{770,2},{771,3},{772,4},{773,5},{774,6},{775,7},{7... | collective-permute-start | bytes 1544 | tf_op jit(solution)/shard_map/ppermute | solution.py:151
  50.0 20.1 %collective-permute-start = (f32[1,128]{1,0:T(1,128)S(1)}, f32[1,128]{1,0:T(1,128)S(1)}, u32[]{:S(2)}, u32[]{:S(2)}) collective-permute-start(f32[1,128]{1,0:T(1,128)S(1)} %bitcast.19), channel_id=1, source_target_pairs={{256,0},{257,1},{258,2},{259,3},{260,4},{261,5},{262,6},{263,7},{2... | collective-permute-start | bytes 1544 | tf_op jit(solution)/shard_map/ppermute | solution.py:151
  70.1 2.6 %collective-permute-start.3 = (f32[1,128]{1,0:T(1,128)S(1)}, f32[1,128]{1,0:T(1,128)S(1)}, u32[]{:S(2)}, u32[]{:S(2)}) collective-permute-start(f32[1,128]{1,0:T(1,128)S(1)} %add_add_fusion), channel_id=1, source_target_pairs={{14,256},{15,257},{12,258},{13,259},{10,260},{11,261},{8,262},{9,2... | collective-permute-start | bytes 1544 | tf_op jit(solution)/shard_map/ppermute | solution.py:151
  72.7 2.6 %collective-permute-start.4 = (f32[1,128]{1,0:T(1,128)S(1)}, f32[1,128]{1,0:T(1,128)S(1)}, u32[]{:S(2)}, u32[]{:S(2)}) collective-permute-start(f32[1,128]{1,0:T(1,128)S(1)} %broadcast_select_fusion), channel_id=1, source_target_pairs={{256,512},{257,513},{258,514},{259,515},{260,516},{261,517},{262,5... | collective-permute-start | bytes 1544 | tf_op jit(solution)/shard_map/ppermute | solution.py:151
  75.3 0.7 collective-permute-start.5

commit v7 on v6

--- a/solution.py
+++ b/solution.py
@@ -20,6 +20,7 @@
     columns, depth = grad_v.shape
     depth //= chunks
     copies = []
+    weight_copy = pltpu.make_async_copy(weight, weight_v, sems.at[2, 0])
     for i in range(chunks):
         part = pl.ds(i * depth, depth)
         copies.append(
@@ -30,10 +31,13 @@
         )
         for copy in copies[-1]:
             copy.start()
-    weight_copy = pltpu.make_async_copy(weight, weight_v, sems.at[2, 0])
-    weight_copy.start()
+        if i == 1:
+            weight_copy.start()
     total = None
     for i in range(chunks):
+        if i == chunks - 1:
+            weight_copy.wait()
+            weight_sq = jnp.sum(weight_v[...] * weight_v[...], axis=(0, 1), keepdims=True)
         for copy in copies[i]:
             copy.wait()
         part = slice(i * depth, (i + 1) * depth)
@@ -42,9 +46,7 @@
         )
         total = term if total is None else total + term
     out[:columns] = total
-    weight_copy.wait()
-    weight_sq = jnp.sum(weight_v[...] * weight_v[...])
-    out[columns:] = jnp.full((out.shape[0] - columns, out.shape[1]), weight_sq, jnp.float32)
+    out[columns:] = jnp.broadcast_to(weight_sq, (out.shape[0] - columns, out.shape[1]))
 
 
 def partial_grad(gradient, projection, weight):
@@ -79,13 +81,13 @@
     )
 
 
-def adam_kernel(total, first, second, projection, new_first, new_second, normal, message):
+def new_moments(low_grad, first, second):
+    return 0.9 * first + 0.1 * low_grad, 0.95 * second + 0.05 * low_grad * low_grad
+
+
+def norm_kernel(total, first, second, projection, normal, message):
     columns = first.shape[0]
-    low_grad = total[:columns]
-    moment = 0.9 * first[...] + 0.1 * low_grad
-    square = 0.95 * second[...] + 0.05 * low_grad * low_grad
-    new_first[...] = moment
-    new_second[...] = square
+    moment, square = new_moments(total[:columns], first[...], second[...])
     first_fix = 1.0 - 0.9**ADAM_STEP
     second_fix = 1.0 - 0.95**ADAM_STEP
     normalized = moment / first_fix / (jnp.sqrt(square / second_fix) + 1e-08)
@@ -98,20 +100,20 @@
         left, left_low = split(projection[i * depth : (i + 1) * depth])
         step = dot_rows(jnp.concatenate([left, left_low, left], axis=1), right)
         squares += jnp.sum((step * step).reshape(depth // SUBLANES, SUBLANES, columns), axis=0)
-    step_sq = jnp.sum(squares)
+    step_sq = jnp.sum(squares, axis=(0, 1), keepdims=True)
     lane = lax.broadcasted_iota(jnp.int32, (1, LANES), 1)
     row = jnp.where(lane == 0, step_sq, total[columns : columns + 1])
     message[...] = jnp.broadcast_to(row[None], message.shape)
 
 
-def adam_and_norm(total, first, second, projection, partners):
+def normal_and_norm(total, first, second, projection, partners):
     vmem = pl.BlockSpec(memory_space=pltpu.VMEM)
     shape = jax.ShapeDtypeStruct(first.shape, jnp.float32)
     return pl.pallas_call(
-        adam_kernel,
-        out_shape=(shape, shape, shape, jax.ShapeDtypeStruct((partners, 1, LANES), jnp.float32)),
+        norm_kernel,
+        out_shape=(shape, jax.ShapeDtypeStruct((partners, 1, LANES), jnp.float32)),
         in_specs=[vmem] * 4,
-        out_specs=(vmem,) * 4,
+        out_specs=(vmem,) * 2,
         compiler_params=pltpu.CompilerParams(vmem_limit_bytes=24 * MIB),
     )(total, first, second, projection)
 
@@ -182,9 +184,9 @@
         total = pair_sum(total, axis)
     total = lax.all_gather(total, "c", axis=0, tiled=True)
 
-    new_first, new_second, normalized, message = adam_and_norm(
-        total, first_moment.T, second_moment.T, projection, lax.axis_size(PLANE)
-    )
+    first, second = first_moment.T, second_moment.T
+    normalized, message = normal_and_norm(total, first, second, projection, lax.axis_size(PLANE))
+    new_first, new_second = new_moments(total[: first.shape[0]], first, second)
     position = lax.axis_index(REPLICA)
     own_projection = lax.dynamic_slice_in_dim(projection, position * rows_here, rows_here, 0)
     step = jnp.dot(

time: 77.1 us -> 77.8 us (level)
  transfers between devices with their start and end apart: 7 -> 7, of which waited for: 4 -> 5; matrix products, arithmetic and copies ran while one was open for 1% -> 2% of each run, Pallas kernels for 0% -> 0%
where the time goes in v7:
time: 77.8 us; the launch traced here: 77.5 us
  blocking collectives  29.5 us (38%)
  waiting for transfers between devices  28.2 us (36%)
  starting transfers between devices  10.6 us (14%)
  Pallas kernels  6.97 us (9%)
  between operations  0.85 us (1%)
  other arithmetic  0.81 us (1%)
    all_gather x4, blocking collectives, pair_sum(): both = lax.all_gather(x, axis, axis=0, tiled=False)  27.7 us
    ppermute x6, waiting for transfers between devices, chip_permute(): return lax.ppermute(x, BLOCKS + REPLICA, pairs)  22 us
    ppermute x6, starting transfers between devices, chip_permute(): return lax.ppermute(x, BLOCKS + REPLICA, pairs)  7.08 us
    all_to_all x1, waiting for transfers between devices, shards(): parts = jnp.sum(lax.all_to_all(message, PLANE, 0, 0), axis=0)  6.23 us
    pallas_call x1, Pallas kernels, partial_grad(): pl.pallas_call(functools.partial(partial_kernel, chunks), out_shape=jax.S...  3.82 us
    all_to_all x1, starting transfers between devices, shards(): parts = jnp.sum(lax.all_to_all(message, PLANE, 0, 0), axis=0)  3.47 us
    pallas_call x1, Pallas kernels, normal_and_norm(): pl.pallas_call(norm_kernel, out_shape=(shape, jax.ShapeDtypeStruct((partn...  2.32 us
    all_gather x1, blocking collectives, shards(): total = lax.all_gather(total, 'c', axis=0, tiled=True)  1.88 us
  transfers between devices with their start and end apart: 7, of which 5 were waited for; matrix products, arithmetic and copies ran while one was open for 2% of the time, Pallas kernels for 0%

profile of v7, /device:TPU:128, one launch (start us, length us, event | category | flops | bytes accessed | tf_op | source)
XLA Modules:
  0.0 77.5 jit_solution(11302104274371732473)
XLA Ops:
  0.6 0.0 copy-start
  0.6 0.0 copy-start.1
  0.7 0.0 copy-start.2
  0.7 3.8 %shard_map.76 = f32[224,128]{1,0:T(8,128)} custom-call(bf16[216,5120]{1,0:T(8,128)(2,1)} %bitcast.26, f32[5120,128]{1,0:T(8,128)} %projection.3, f32[320,216]{1,0:T(8,128)} %weight.1), custom_call_target="tpu_custom_call" | custom-call | tf_op jit(solution)/shard_map/pallas_call | solution.py:57
  4.5 2.2 %all-gather = f32[448,128]{1,0:T(8,128)S(1)} all-gather(f32[224,128]{1,0:T(8,128)} %shard_map.76), channel_id=2, replica_groups=mesh['h1'=2,'h0'=2,'y1'=2,'y0'=2,'x1'=2,'x0'=2,'l2'=2,'l1'=2,'l0'=2,'c'=..., dimensions={0}, use_global_device_ids=true | all-gather | bytes 344064 | tf_op jit(solution)/shard_map/all_gather | solution.py:139
  6.7 4.9 %all-gather.2 = f32[224,128]{1,0:T(8,128)S(1)} all-gather(f32[112,128]{1,0:T(8,128)S(1)} %dynamic-slice_add_fusion), channel_id=4, replica_groups=mesh['h1'=2,'h0'=2,'y1'=2,'y0'=2,'x1'=2,'x0'=2,'l2'=2,'l1'=2,'l0'=2,'c'=..., dimensions={0}, use_global_device_ids=true | all-gather | bytes 172032 | tf_op jit(solution)/shard_map/all_gather | solution.py:139
  11.6 6.4 %all_gather.24 = f32[2,112,128]{2,1,0:T(8,128)S(1)} all-gather(f32[1,112,128]{2,1,0:T(8,128)S(1)} %fusion.4), channel_id=1, replica_groups=mesh['h1'=2,'h0'=2,'y1'=2,'y0'=2,'x1'=2,'x0'=2,'l2'=2,'l1'=2,'l0'=2,'c'=..., dimensions={0}, use_global_device_ids=true | all-gather | bytes 172032 | tf_op jit(solution)/shard_map/all_gather | solution.py:139
  18.0 14.3 %all_gather.25 = f32[2,112,128]{2,1,0:T(8,128)S(1)} all-gather(f32[1,112,128]{2,1,0:T(8,128)S(1)} %slice_add_fusion.1), channel_id=1, replica_groups=mesh['h1'=2,'h0'=2,'y1'=2,'y0'=2,'x1'=2,'x0'=2,'l2'=2,'l1'=2,'l0'=2,'c'=..., dimensions={0}, use_global_device_ids=true | all-gather | bytes 172032 | tf_op jit(solution)/shard_map/all_gather | solution.py:139
  32.2 1.9 %all-gather.1 = f32[1,224,128]{2,1,0:T(8,128)S(1)} all-gather(f32[1,112,128]{2,1,0:T(8,128)S(1)} %slice_add_fusion), channel_id=3, replica_groups=mesh['h1'=2,'h0'=2,'y1'=2,'y0'=2,'x1'=2,'x0'=2,'l2'=2,'l1'=2,'l0'=2,'c'=..., dimensions={1}, use_global_device_ids=true | all-gather | bytes 172032 | tf_op jit(solution)/shard_map/all_gather | solution.py:185
  34.1 0.0 copy-done
  34.1 0.0 copy-done.1
  34.1 0.0 copy-done.2
  34.1 2.3 %shard_map.77 = (f32[216,128]{1,0:T(8,128)S(1)}, f32[16,1,128]{2,1,0:T(1,128)}) custom-call(f32[224,128]{1,0:T(8,128)S(1)} %bitcast.23, f32[216,128]{1,0:T(8,128)S(1)} %bitcast.24, f32[216,128]{1,0:T(8,128)S(1)} %bitcast.25, f32[5120,128]{1,0:T(8,128)S(1)} %copy-done), custom_call_target="tpu_custom_call" | custom-call | tf_op jit(solution)/shard_map/pallas_call | solution.py:112
  36.4 3.5 %all-to-all-start = ((f32[16,1,128]{2,1,0:T(1,128)}), f32[16,1,128]{2,1,0:T(1,128)S(1)}, u32[]{:S(2)}, u32[]{:S(2)}) async-start(f32[16,1,128]{2,1,0:T(1,128)} %get-tuple-element.5), calls=%async_computation | async-start | bytes 16384 | tf_op jit(solution)/shard_map/all_to_all | solution.py:195
  39.9 0.7 fusion.3
  40.6 0.5 fusion.step
  41.1 6.2 %all-to-all-done = f32[16,1,128]{2,1,0:T(1,128)S(1)} async-done(((f32[16,1,128]{2,1,0:T(1,128)}), f32[16,1,128]{2,1,0:T(1,128)S(1)}, u32[]{:S(2)}, u32[]{:S(2)}) %all-to-all-start) | async-done | bytes 8224 | tf_op jit(solution)/shard_map/all_to_all | solution.py:195
  47.4 1.3 %collective-permute-start = (f32[1,128]{1,0:T(1,128)S(1)}, f32[1,128]{1,0:T(1,128)S(1)}, u32[]{:S(2)}, u32[]{:S(2)}) collective-permute-start(f32[1,128]{1,0:T(1,128)S(1)} %bitcast.27), channel_id=1, source_target_pairs={{256,0},{257,1},{258,2},{259,3},{260,4},{261,5},{262,6},{263,7},{2... | collective-permute-start | bytes 1544 | tf_op jit(solution)/shard_map/ppermute | solution.py:153
  48.7 1.3 %collective-permute-start.1 = (f32[1,128]{1,0:T(1,128)S(1)}, f32[1,128]{1,0:T(1,128)S(1)}, u32[]{:S(2)}, u32[]{:S(2)}) collective-permute-start(f32[1,128]{1,0:T(1,128)S(1)} %bitcast.28), channel_id=1, source_target_pairs={{512,14},{513,15},{514,12},{515,13},{516,10},{517,11},{518,8},{519... | collective-permute-start | bytes 1544 | tf_op jit(solution)/shard_map/ppermute | solution.py:153
  50.0 1.3 %collective-permute-start.2 = (f32[1,128]{1,0:T(1,128)S(1)}, f32[1,128]{1,0:T(1,128)S(1)}, u32[]{:S(2)}, u32[]{:S(2)}) collective-permute-start(f32[1,128]{1,0:T(1,128)S(1)} %bitcast.29), channel_id=1, source_target_pairs={{768,0},{769,1},{770,2},{771,3},{772,4},{773,5},{774,6},{775,7},{7... | collective-permute-start | bytes 1544 | tf_op jit(solution)/shard_map/ppermute | solution.py:153
  51.3 10.9 %collective-permute-done = f32[1,128]{1,0:T(1,128)S(1)} collective-permute-done((f32[1,128]{1,0:T(1,128)S(1)}, f32[1,128]{1,0:T(1,128)S(1)}, u32[]{:S(2)}, u32[]{:S(2)}) %collective-permute-start) | collective-permute-done | bytes 544 | tf_op jit(solution)/shard_map/ppermute | solution.py:153
  62.2 8.6 %collective-permute-done.1 = f32[1,128]{1,0:T(1,128)S(1)} collective-permute-done((f32[1,128]{1,0:T(1,128)S(1)}, f32[1,128]{1,0:T(1,128)S(1)}, u32[]{:S(2)}, u32[]{:S(2)}) %collective-permute-start.1) | collective-permute-done | bytes 544 | tf_op jit(solution)/shard_map/ppermute | solution.py:153
  70.8 0.0 collective-permute-done.2
  70.8 1.3 %collective-permute-start.3 = (f32[1,128]{1,0:T(1,128)S(1)}, f32[1,128]{1,0:T(1,128)S(1)}, u32[]{:S(2)}, u32[]{:S(2)}) collective-permute-start(f32[1,128]{1,0:T(1,128)S(1)} %add_add_fusion), channel_id=1, source_target_pairs={{14,256},{15,257},{12,258},{13,259},{10,260},{11,261},{8,262},{9,2... | collective-permute-start | bytes 1544 | tf_op jit(solution)/shard_map/ppermute | solution.py:153
  72.1 1.3 %collective-permute-done.3 = f32[1,128]{1,0:T(1,128)S(1)} collective-permute-done((f32[1,128]{1,0:T(1,128)S(1)}, f32[1,128]{1,0:T(1,128)S(1)}, u32[]{:S(2)}, u32[]{:S(2)}) %collective-permute-start.3) | collective-permute-done | bytes 544 | tf_op jit(solution)/shard_map/ppermute | solution.py:153
  73.4 1.3 %collective-permute-start.4 = (f32[1,128]{1,0:T(1,128)S(1)}, f32[1,128]{1,0:T(1,128)S(1)}, u32[]{:S(2)}, u32[]{:S(2)}) collective-permute-start(f32[1,128]{1,0:T(1,128)S(1)} %broadcast_select_fusion), channel_id=1, source_target_pairs={{256,512},{257,513},{258,514},{259,515},{260,516},{261,517},{262,5... | collective-permute-start | bytes 1544 | tf_op jit(solution)/shard_map/ppermute | solution.py:153
  74.7 1.3 %collective-permute-done.4 = f32[1,128]{1,0:T(1,128)S(1)} collective-permute-done((f32[1,128]{1,0:T(1,128)S(1)}, f32[1,128]{1,0:T(1,128)S(1)}, u32[]{:S(2)}, u32[]{:S(2)}) %collective-permute-start.4) | collective-permute-done | bytes 544 | tf_op jit(solution)/shard_map/ppermute | solution.py:153
  75.9 0.6 collective-permute-start.5
  76.6 0.0 collective-permute-done.5
  76.6 0.8 %shard_map.78 = f32[320,216]{1,0:T(8,128)} custom-call(f32[1,128]{1,0:T(1,128)S(1)} %broadcast_select_fusion.2.sums, f32[320,216]{1,0:T(8,128)S(1)} %fusion.step), custom_call_target="tpu_custom_call" | custom-call | tf_op jit(solution)/shard_map/pallas_call | solution.py:129
  (10 shorter events, 0.1 us)
Async XLA Ops:
  0.6 33.5 %copy-start = (f32[5120,128]{1,0:T(8,128)S(1)}, f32[5120,128]{1,0:T(8,128)}, u32[]{:S(2)}) copy-start(f32[5120,128]{1,0:T(8,128)} %projection.3) | copy-start | bytes 7864324
  0.6 33.5 %copy-start.1 = (f32[128,216]{0,1:T(8,128)S(1)}, f32[128,216]{0,1:T(8,128)}, u32[]{:S(2)}) copy-start(f32[128,216]{0,1:T(8,128)} %param.7) | copy-start | bytes 331780
  0.7 33.5 %copy-start.2 = (f32[128,216]{0,1:T(8,128)S(1)}, f32[128,216]{0,1:T(8,128)}, u32[]{:S(2)}) copy-start(f32[128,216]{0,1:T(8,128)} %param.8) | copy-start | bytes 331780
  36.4 10.9 %all-to-all-start = ((f32[16,1,128]{2,1,0:T(1,128)}), f32[16,1,128]{2,1,0:T(1,128)S(1)}, u32[]{:S(2)}, u32[]{:S(2)}) async-start(f32[16,1,128]{2,1,0:T(1,128)} %get-tuple-element.5), calls=%async_computation | async-start | bytes 16384 | tf_op jit(solution)/shard_map/all_to_all | solution.py:195
  47.4 14.8 %collective-permute-start = (f32[1,128]{1,0:T(1,128)S(1)}, f32[1,128]{1,0:T(1,128)S(1)}, u32[]{:S(2)}, u32[]{:S(2)}) collective-permute-start(f32[1,128]{1,0:T(1,128)S(1)} %bitcast.27), channel_id=1, source_target_pairs={{256,0},{257,1},{258,2},{259,3},{260,4},{261,5},{262,6},{263,7},{2... | collective-permute-start | bytes 1544 | tf_op jit(solution)/shard_map/ppermute | solution.py:153
  48.7 22.1 %collective-permute-start.1 = (f32[1,128]{1,0:T(1,128)S(1)}, f32[1,128]{1,0:T(1,128)S(1)}, u32[]{:S(2)}, u32[]{:S(2)}) collective-permute-start(f32[1,128]{1,0:T(1,128)S(1)} %bitcast.28), channel_id=1, source_target_pairs={{512,14},{513,15},{514,12},{515,13},{516,10},{517,11},{518,8},{519... | collective-permute-start | bytes 1544 | tf_op jit(solution)/shard_map/ppermute | solution.py:153
  50.0 20.8 %collective-permute-start.2 = (f32[1,128]{1,0:T(1,128)S(1)}, f32[1,128]{1,0:T(1,128)S(1)}, u32[]{:S(2)}, u32[]{:S(2)}) collective-permute-start(f32[1,128]{1,0:T(1,128)S(1)} %bitcast.29), channel_id=1, source_target_pairs={{768,0},{769,1},{770,2},{771,3},{772,4},{773,5},{774,6},{775,7},{7... | collective-permute-start | bytes 1544 | tf_op jit(solution)/shard_map/ppermute | solution.py:153
  70.8 2.6 %collective-permute-start.3 = (f32[1,128]{1,0:T(1,128)S(1)}, f32[1,128]{1,0:T(1,128)S(1)}, u32[]{:S(2)}, u32[]{:S(2)}) collective-permute-start(f32[1,128]{1,0:T(1,128)S(1)} %add_add_fusion), channel_id=1, source_target_pairs={{14,256},{15,257},{12,258},{13,259},{10,260},{11,261},{8,262},{9,2... | collective-permute-start | bytes 1544 | tf_op jit(solution)/shard_map/ppermute | solution.py:153
  73.4 2.6 %collective-permute-start.4 = (f32[1,128]{1,0:T(1,128)S(1)}, f32[1,128]{1,0:T(1,128)S(1)}, u32[]{:S(2)}, u32[]{:S(2)}) collective-permute-start(f32[1,128]{1,0:T(1,128)S(1)} %broadcast_select_fusion), channel_id=1, source_target_pairs={{256,512},{257,513},{258,514},{259,515},{260,516},{261,517},{262,5... | collective-permute-start | bytes 1544 | tf_op jit(solution)/shard_map/ppermute | solution.py:153
  75.9 0.7 collective-permute-start.5

commit v8 on v7

--- a/solution.py
+++ b/solution.py
@@ -162,7 +162,7 @@
     half = chips // 2
     mirrored = [(2 * chips + i, chips - 1 - i) for i in range(chips)]
     total = x
-    for moves in (run(chips, 0, chips), mirrored, run(3 * chips, 0, chips)):
+    for moves in (mirrored, run(3 * chips, 0, chips), run(chips, 0, chips)):
         total = total + chip_permute(x, moves)
     place = lax.axis_index(BLOCKS + REPLICA[:3])
     for moves in SPREAD:

time: 77.8 us -> 77.1 us (level)
  transfers between devices with their start and end apart: 7 -> 7, of which waited for: 5 -> 4; matrix products, arithmetic and copies ran while one was open for 2% -> 2% of each run, Pallas kernels for 0% -> 0%
where the time goes in v8:
time: 77.1 us; the launch traced here: 76.8 us
  blocking collectives  29.5 us (38%)
  waiting for transfers between devices  27.6 us (36%)
  starting transfers between devices  10.6 us (14%)
  Pallas kernels  6.97 us (9%)
  between operations  0.86 us (1%)
  other arithmetic  0.81 us (1%)
    all_gather x4, blocking collectives, pair_sum(): both = lax.all_gather(x, axis, axis=0, tiled=False)  27.7 us
    ppermute x6, waiting for transfers between devices, chip_permute(): return lax.ppermute(x, BLOCKS + REPLICA, pairs)  21.4 us
    ppermute x6, starting transfers between devices, chip_permute(): return lax.ppermute(x, BLOCKS + REPLICA, pairs)  7.08 us
    all_to_all x1, waiting for transfers between devices, shards(): parts = jnp.sum(lax.all_to_all(message, PLANE, 0, 0), axis=0)  6.23 us
    pallas_call x1, Pallas kernels, partial_grad(): pl.pallas_call(functools.partial(partial_kernel, chunks), out_shape=jax.S...  3.82 us
    all_to_all x1, starting transfers between devices, shards(): parts = jnp.sum(lax.all_to_all(message, PLANE, 0, 0), axis=0)  3.47 us
    pallas_call x1, Pallas kernels, normal_and_norm(): pl.pallas_call(norm_kernel, out_shape=(shape, jax.ShapeDtypeStruct((partn...  2.32 us
    all_gather x1, blocking collectives, shards(): total = lax.all_gather(total, 'c', axis=0, tiled=True)  1.88 us
  transfers between devices with their start and end apart: 7, of which 4 were waited for; matrix products, arithmetic and copies ran while one was open for 2% of the time, Pallas kernels for 0%

profile of v8, /device:TPU:128, one launch (start us, length us, event | category | flops | bytes accessed | tf_op | source)
XLA Modules:
  0.0 76.8 jit_solution(3780585098972320674)
XLA Ops:
  0.6 0.0 copy-start
  0.6 0.0 copy-start.1
  0.7 0.0 copy-start.2
  0.7 3.8 %shard_map.76 = f32[224,128]{1,0:T(8,128)} custom-call(bf16[216,5120]{1,0:T(8,128)(2,1)} %bitcast.26, f32[5120,128]{1,0:T(8,128)} %projection.3, f32[320,216]{1,0:T(8,128)} %weight.1), custom_call_target="tpu_custom_call" | custom-call | tf_op jit(solution)/shard_map/pallas_call | solution.py:57
  4.5 2.2 %all-gather = f32[448,128]{1,0:T(8,128)S(1)} all-gather(f32[224,128]{1,0:T(8,128)} %shard_map.76), channel_id=2, replica_groups=mesh['h1'=2,'h0'=2,'y1'=2,'y0'=2,'x1'=2,'x0'=2,'l2'=2,'l1'=2,'l0'=2,'c'=..., dimensions={0}, use_global_device_ids=true | all-gather | bytes 344064 | tf_op jit(solution)/shard_map/all_gather | solution.py:139
  6.7 4.9 %all-gather.2 = f32[224,128]{1,0:T(8,128)S(1)} all-gather(f32[112,128]{1,0:T(8,128)S(1)} %dynamic-slice_add_fusion), channel_id=4, replica_groups=mesh['h1'=2,'h0'=2,'y1'=2,'y0'=2,'x1'=2,'x0'=2,'l2'=2,'l1'=2,'l0'=2,'c'=..., dimensions={0}, use_global_device_ids=true | all-gather | bytes 172032 | tf_op jit(solution)/shard_map/all_gather | solution.py:139
  11.6 6.4 %all_gather.24 = f32[2,112,128]{2,1,0:T(8,128)S(1)} all-gather(f32[1,112,128]{2,1,0:T(8,128)S(1)} %fusion.4), channel_id=1, replica_groups=mesh['h1'=2,'h0'=2,'y1'=2,'y0'=2,'x1'=2,'x0'=2,'l2'=2,'l1'=2,'l0'=2,'c'=..., dimensions={0}, use_global_device_ids=true | all-gather | bytes 172032 | tf_op jit(solution)/shard_map/all_gather | solution.py:139
  18.0 14.3 %all_gather.25 = f32[2,112,128]{2,1,0:T(8,128)S(1)} all-gather(f32[1,112,128]{2,1,0:T(8,128)S(1)} %slice_add_fusion.1), channel_id=1, replica_groups=mesh['h1'=2,'h0'=2,'y1'=2,'y0'=2,'x1'=2,'x0'=2,'l2'=2,'l1'=2,'l0'=2,'c'=..., dimensions={0}, use_global_device_ids=true | all-gather | bytes 172032 | tf_op jit(solution)/shard_map/all_gather | solution.py:139
  32.2 1.9 %all-gather.1 = f32[1,224,128]{2,1,0:T(8,128)S(1)} all-gather(f32[1,112,128]{2,1,0:T(8,128)S(1)} %slice_add_fusion), channel_id=3, replica_groups=mesh['h1'=2,'h0'=2,'y1'=2,'y0'=2,'x1'=2,'x0'=2,'l2'=2,'l1'=2,'l0'=2,'c'=..., dimensions={1}, use_global_device_ids=true | all-gather | bytes 172032 | tf_op jit(solution)/shard_map/all_gather | solution.py:185
  34.1 0.0 copy-done
  34.1 0.0 copy-done.1
  34.1 0.0 copy-done.2
  34.1 2.3 %shard_map.77 = (f32[216,128]{1,0:T(8,128)S(1)}, f32[16,1,128]{2,1,0:T(1,128)}) custom-call(f32[224,128]{1,0:T(8,128)S(1)} %bitcast.23, f32[216,128]{1,0:T(8,128)S(1)} %bitcast.24, f32[216,128]{1,0:T(8,128)S(1)} %bitcast.25, f32[5120,128]{1,0:T(8,128)S(1)} %copy-done), custom_call_target="tpu_custom_call" | custom-call | tf_op jit(solution)/shard_map/pallas_call | solution.py:112
  36.4 3.5 %all-to-all-start = ((f32[16,1,128]{2,1,0:T(1,128)}), f32[16,1,128]{2,1,0:T(1,128)S(1)}, u32[]{:S(2)}, u32[]{:S(2)}) async-start(f32[16,1,128]{2,1,0:T(1,128)} %get-tuple-element.5), calls=%async_computation | async-start | bytes 16384 | tf_op jit(solution)/shard_map/all_to_all | solution.py:195
  39.9 0.7 fusion.3
  40.6 0.5 fusion.step
  41.1 6.2 %all-to-all-done = f32[16,1,128]{2,1,0:T(1,128)S(1)} async-done(((f32[16,1,128]{2,1,0:T(1,128)}), f32[16,1,128]{2,1,0:T(1,128)S(1)}, u32[]{:S(2)}, u32[]{:S(2)}) %all-to-all-start) | async-done | bytes 8224 | tf_op jit(solution)/shard_map/all_to_all | solution.py:195
  47.4 1.3 %collective-permute-start = (f32[1,128]{1,0:T(1,128)S(1)}, f32[1,128]{1,0:T(1,128)S(1)}, u32[]{:S(2)}, u32[]{:S(2)}) collective-permute-start(f32[1,128]{1,0:T(1,128)S(1)} %bitcast.27), channel_id=1, source_target_pairs={{512,14},{513,15},{514,12},{515,13},{516,10},{517,11},{518,8},{519... | collective-permute-start | bytes 1544 | tf_op jit(solution)/shard_map/ppermute | solution.py:153
  48.7 1.3 %collective-permute-start.1 = (f32[1,128]{1,0:T(1,128)S(1)}, f32[1,128]{1,0:T(1,128)S(1)}, u32[]{:S(2)}, u32[]{:S(2)}) collective-permute-start(f32[1,128]{1,0:T(1,128)S(1)} %bitcast.28), channel_id=1, source_target_pairs={{768,0},{769,1},{770,2},{771,3},{772,4},{773,5},{774,6},{775,7},{7... | collective-permute-start | bytes 1544 | tf_op jit(solution)/shard_map/ppermute | solution.py:153
  50.0 1.3 %collective-permute-start.2 = (f32[1,128]{1,0:T(1,128)S(1)}, f32[1,128]{1,0:T(1,128)S(1)}, u32[]{:S(2)}, u32[]{:S(2)}) collective-permute-start(f32[1,128]{1,0:T(1,128)S(1)} %bitcast.29), channel_id=1, source_target_pairs={{256,0},{257,1},{258,2},{259,3},{260,4},{261,5},{262,6},{263,7},{2... | collective-permute-start | bytes 1544 | tf_op jit(solution)/shard_map/ppermute | solution.py:153
  51.3 18.8 %collective-permute-done = f32[1,128]{1,0:T(1,128)S(1)} collective-permute-done((f32[1,128]{1,0:T(1,128)S(1)}, f32[1,128]{1,0:T(1,128)S(1)}, u32[]{:S(2)}, u32[]{:S(2)}) %collective-permute-start) | collective-permute-done | bytes 544 | tf_op jit(solution)/shard_map/ppermute | solution.py:153
  70.1 0.0 collective-permute-done.1
  70.1 0.0 collective-permute-done.2
  70.1 1.3 %collective-permute-start.3 = (f32[1,128]{1,0:T(1,128)S(1)}, f32[1,128]{1,0:T(1,128)S(1)}, u32[]{:S(2)}, u32[]{:S(2)}) collective-permute-start(f32[1,128]{1,0:T(1,128)S(1)} %add_add_fusion), channel_id=1, source_target_pairs={{14,256},{15,257},{12,258},{13,259},{10,260},{11,261},{8,262},{9,2... | collective-permute-start | bytes 1544 | tf_op jit(solution)/shard_map/ppermute | solution.py:153
  71.4 1.3 %collective-permute-done.3 = f32[1,128]{1,0:T(1,128)S(1)} collective-permute-done((f32[1,128]{1,0:T(1,128)S(1)}, f32[1,128]{1,0:T(1,128)S(1)}, u32[]{:S(2)}, u32[]{:S(2)}) %collective-permute-start.3) | collective-permute-done | bytes 544 | tf_op jit(solution)/shard_map/ppermute | solution.py:153
  72.7 1.3 %collective-permute-start.4 = (f32[1,128]{1,0:T(1,128)S(1)}, f32[1,128]{1,0:T(1,128)S(1)}, u32[]{:S(2)}, u32[]{:S(2)}) collective-permute-start(f32[1,128]{1,0:T(1,128)S(1)} %broadcast_select_fusion), channel_id=1, source_target_pairs={{256,512},{257,513},{258,514},{259,515},{260,516},{261,517},{262,5... | collective-permute-start | bytes 1544 | tf_op jit(solution)/shard_map/ppermute | solution.py:153
  74.0 1.3 %collective-permute-done.4 = f32[1,128]{1,0:T(1,128)S(1)} collective-permute-done((f32[1,128]{1,0:T(1,128)S(1)}, f32[1,128]{1,0:T(1,128)S(1)}, u32[]{:S(2)}, u32[]{:S(2)}) %collective-permute-start.4) | collective-permute-done | bytes 544 | tf_op jit(solution)/shard_map/ppermute | solution.py:153
  75.3 0.6 collective-permute-start.5
  75.9 0.0 collective-permute-done.5
  76.0 0.8 %shard_map.78 = f32[320,216]{1,0:T(8,128)} custom-call(f32[1,128]{1,0:T(1,128)S(1)} %broadcast_select_fusion.2.sums, f32[320,216]{1,0:T(8,128)S(1)} %fusion.step), custom_call_target="tpu_custom_call" | custom-call | tf_op jit(solution)/shard_map/pallas_call | solution.py:129
  (10 shorter events, 0.1 us)
Async XLA Ops:
  0.6 33.5 %copy-start = (f32[5120,128]{1,0:T(8,128)S(1)}, f32[5120,128]{1,0:T(8,128)}, u32[]{:S(2)}) copy-start(f32[5120,128]{1,0:T(8,128)} %projection.3) | copy-start | bytes 7864324
  0.6 33.5 %copy-start.1 = (f32[128,216]{0,1:T(8,128)S(1)}, f32[128,216]{0,1:T(8,128)}, u32[]{:S(2)}) copy-start(f32[128,216]{0,1:T(8,128)} %param.7) | copy-start | bytes 331780
  0.7 33.5 %copy-start.2 = (f32[128,216]{0,1:T(8,128)S(1)}, f32[128,216]{0,1:T(8,128)}, u32[]{:S(2)}) copy-start(f32[128,216]{0,1:T(8,128)} %param.8) | copy-start | bytes 331780
  36.4 10.9 %all-to-all-start = ((f32[16,1,128]{2,1,0:T(1,128)}), f32[16,1,128]{2,1,0:T(1,128)S(1)}, u32[]{:S(2)}, u32[]{:S(2)}) async-start(f32[16,1,128]{2,1,0:T(1,128)} %get-tuple-element.5), calls=%async_computation | async-start | bytes 16384 | tf_op jit(solution)/shard_map/all_to_all | solution.py:195
  47.4 22.7 %collective-permute-start = (f32[1,128]{1,0:T(1,128)S(1)}, f32[1,128]{1,0:T(1,128)S(1)}, u32[]{:S(2)}, u32[]{:S(2)}) collective-permute-start(f32[1,128]{1,0:T(1,128)S(1)} %bitcast.27), channel_id=1, source_target_pairs={{512,14},{513,15},{514,12},{515,13},{516,10},{517,11},{518,8},{519... | collective-permute-start | bytes 1544 | tf_op jit(solution)/shard_map/ppermute | solution.py:153
  48.7 21.4 %collective-permute-start.1 = (f32[1,128]{1,0:T(1,128)S(1)}, f32[1,128]{1,0:T(1,128)S(1)}, u32[]{:S(2)}, u32[]{:S(2)}) collective-permute-start(f32[1,128]{1,0:T(1,128)S(1)} %bitcast.28), channel_id=1, source_target_pairs={{768,0},{769,1},{770,2},{771,3},{772,4},{773,5},{774,6},{775,7},{7... | collective-permute-start | bytes 1544 | tf_op jit(solution)/shard_map/ppermute | solution.py:153
  50.0 20.1 %collective-permute-start.2 = (f32[1,128]{1,0:T(1,128)S(1)}, f32[1,128]{1,0:T(1,128)S(1)}, u32[]{:S(2)}, u32[]{:S(2)}) collective-permute-start(f32[1,128]{1,0:T(1,128)S(1)} %bitcast.29), channel_id=1, source_target_pairs={{256,0},{257,1},{258,2},{259,3},{260,4},{261,5},{262,6},{263,7},{2... | collective-permute-start | bytes 1544 | tf_op jit(solution)/shard_map/ppermute | solution.py:153
  70.1 2.6 %collective-permute-start.3 = (f32[1,128]{1,0:T(1,128)S(1)}, f32[1,128]{1,0:T(1,128)S(1)}, u32[]{:S(2)}, u32[]{:S(2)}) collective-permute-start(f32[1,128]{1,0:T(1,128)S(1)} %add_add_fusion), channel_id=1, source_target_pairs={{14,256},{15,257},{12,258},{13,259},{10,260},{11,261},{8,262},{9,2... | collective-permute-start | bytes 1544 | tf_op jit(solution)/shard_map/ppermute | solution.py:153
  72.7 2.6 %collective-permute-start.4 = (f32[1,128]{1,0:T(1,128)S(1)}, f32[1,128]{1,0:T(1,128)S(1)}, u32[]{:S(2)}, u32[]{:S(2)}) collective-permute-start(f32[1,128]{1,0:T(1,128)S(1)} %broadcast_select_fusion), channel_id=1, source_target_pairs={{256,512},{257,513},{258,514},{259,515},{260,516},{261,517},{262,5... | collective-permute-start | bytes 1544 | tf_op jit(solution)/shard_map/ppermute | solution.py:153
  75.3 0.7 collective-permute-start.5
